TPU v7x, 32 devices: a whole 2x2x4 slice. The times are simulated.
32 devices in a mesh: ctx: 16 (over z, x, core), tp: 2 (over y).
Axes of the slice: x: 2, y: 2, z: 4, core: 2. Of those that a mesh axis runs over, the one named last changes fastest.
Arguments:
- tokens: bfloat16 [2048, 2048], P('ctx'), may hold values from -6 to 6
- block_order: int32 [32], replicated, may hold values from 0 to 31, each once
- ln_gain: float32 [2048], replicated, may hold values from 0.1 to 1.9
- ln_bias: float32 [2048], replicated, may hold values from -1.8 to 1.8
- qkv_weight: bfloat16 [2048, 3, 2048], P('ctx', None, 'tp'), may hold values from -0.125 to 0.125
- qkv_bias: float32 [3, 2048], P(None, 'tp'), may hold values from -3 to 3
- out_weight: bfloat16 [2048, 2048], P('ctx', 'tp'), may hold values from -0.5 to 0.5
- fc1_weight: bfloat16 [2048, 8192], P('ctx', 'tp'), may hold values from -0.125 to 0.125
- fc1_bias: float32 [8192], P('tp'), may hold values from -3 to 3
- fc2_weight: bfloat16 [2048, 8192], P('ctx', 'tp'), may hold values from -0.09375 to 0.09375
- out_bias: float32 [2048], replicated, may hold values from -3 to 3
- cotangent: bfloat16 [2048, 2048], P('ctx'), may hold values from -6 to 6
Outputs:
- output: float32 [2048, 2048], P('ctx')
- input_grad: float32 [2048, 2048], P('ctx')
- ln_gain_grad: float32 [2048], replicated
- ln_bias_grad: float32 [2048], replicated
- qkv_weight_grad: float32 [2048, 3, 2048], P('ctx', None, 'tp')
- qkv_bias_grad: float32 [3, 2048], P(None, 'tp')
- out_weight_grad: float32 [2048, 2048], P('ctx', 'tp')
- fc1_weight_grad: float32 [2048, 8192], P('ctx', 'tp')
- fc1_bias_grad: float32 [8192], P('tp')
- fc2_weight_grad: float32 [2048, 8192], P('ctx', 'tp')
- out_bias_grad: float32 [2048], replicated
Inputs may be any that keep to these rules, and one draw needn't show every extreme that they name: block_order is a permutation: each of the 32 half-blocks of 64 positions is held by exactly one pair of rows.
All inputs are finite; a program needn't handle non-finite values.
Results may differ from a plain program's by a relative error of at most 0.015.
Values may be sent and summed in bfloat16 or wider, within the bound.
A program may use at most 256 MiB of HBM per device.

v0:
```python
import functools
import math

import jax
import jax.numpy as jnp
from jax import lax
from jax.experimental import pallas as pl
from jax.experimental.pallas import tpu as pltpu
from jax.sharding import PartitionSpec as P

HEAD = 64
ROT = 32
EPS = 1e-05
NEG = -1e30
BF = jnp.bfloat16
F32 = jnp.float32
NN = (((1,), (0,)), ((), ()))
NT = (((1,), (1,)), ((), ()))
TN = (((0,), (0,)), ((), ()))


def mm(left, right, dims=NN):
    return lax.dot_general(left, right, dims, preferred_element_type=F32)


def tables(positions, width):
    freqs = 10000.0 ** (-(jnp.arange(width // 2, dtype=F32) * 2.0) / width)
    angles = positions.astype(F32)[:, None] * freqs[None, :]
    return (jnp.cos(angles), jnp.sin(angles))


def turned(value, cosine, sine):
    half = cosine.shape[-1]
    first, second = value[..., :half], value[..., half : 2 * half]
    return jnp.concatenate(
        [first * cosine - second * sine, second * cosine + first * sine, value[..., 2 * half :]],
        axis=-1,
    )


def attention_blocks(own_place, places, mixed, grad_att, gather, scatter):
    count, width = grad_att.shape[0], grad_att.shape[1] // 4
    heads = width // HEAD
    scale = 1.0 / math.sqrt(HEAD)
    grad_att = grad_att[:, 3 * width :].astype(BF)
    cosine, sine = tables(own_place, ROT)
    cosine, sine = cosine[:, None, :], sine[:, None, :]
    kinds = [mixed[:, kind * width : (kind + 1) * width].reshape(count, heads, HEAD) for kind in range(3)]
    queries = turned(kinds[0], cosine, sine).astype(BF)
    keys = gather(turned(kinds[1], cosine, sine).astype(BF))
    values = gather(kinds[2].astype(BF))
    grad_att = grad_att.reshape(count, heads, HEAD)
    block = math.gcd(128, count)

    def one(at, carry):
        key_grad, value_grad, attended, query_grad = carry
        query = lax.dynamic_slice_in_dim(queries, at * block, block)
        grad = lax.dynamic_slice_in_dim(grad_att, at * block, block)
        place = lax.dynamic_slice_in_dim(own_place, at * block, block)
        visible = (place[:, None] >= places[None, :])[None]
        scores = jnp.einsum("qhe,khe->hqk", query, keys, preferred_element_type=F32) * scale
        scores = jnp.where(visible, scores, NEG)
        top = jnp.max(scores, axis=-1, keepdims=True)
        expo = jnp.where(visible, jnp.exp(scores - top), 0.0)
        total = jnp.sum(expo, axis=-1)
        summed = jnp.einsum("hqk,khe->qhe", expo.astype(BF), values, preferred_element_type=F32)
        attend = summed / jnp.transpose(total)[..., None]
        delta = jnp.transpose(jnp.sum(grad.astype(F32) * attend, axis=-1))
        prob = expo / total[..., None]
        dprob = jnp.einsum("qhe,khe->hqk", grad, values, preferred_element_type=F32)
        dscore = (prob * (dprob - delta[..., None])).astype(BF)
        part_q = jnp.einsum("hqk,khe->qhe", dscore, keys, preferred_element_type=F32) * scale
        key_grad += jnp.einsum("hqk,qhe->khe", dscore, query, preferred_element_type=F32) * scale
        value_grad += jnp.einsum("hqk,qhe->khe", prob.astype(BF), grad, preferred_element_type=F32)
        attended = lax.dynamic_update_slice_in_dim(attended, attend.astype(BF), at * block, 0)
        query_grad = lax.dynamic_update_slice_in_dim(query_grad, part_q, at * block, 0)
        return (key_grad, value_grad, attended, query_grad)

    zeros = jnp.zeros(keys.shape, F32)
    own = jnp.zeros((count, heads, HEAD), F32)
    key_grad, value_grad, attended, query_grad = lax.fori_loop(
        0, count // block, one, (zeros, zeros, own.astype(BF), own)
    )
    key_grad, value_grad = scatter(key_grad), scatter(value_grad)
    grad_mixed = jnp.concatenate(
        [
            turned(query_grad, cosine, -sine).astype(BF).reshape(count, width),
            turned(key_grad, cosine, -sine).astype(BF).reshape(count, width),
            value_grad.astype(BF).reshape(count, width),
            jnp.zeros((count, width), BF),
        ],
        axis=1,
    )
    attended = jnp.concatenate(
        [jnp.zeros((count, 3 * width), BF), attended.reshape(count, width)], axis=1
    )
    return attended, grad_mixed


MESH = pl.DeviceIdType.MESH
UP, DOWN, ACROSS, OTHER, CORE = range(5)


def at_rows(start, size):
    return pl.ds(pl.multiple_of(start, size), size)


def remote(source, target, send, receive, device):
    return pltpu.make_async_remote_copy(
        src_ref=source, dst_ref=target, send_sem=send, recv_sem=receive, device_id=device,
        device_id_type=MESH,
    )


class Place:
    def __init__(self, line):
        self.line = line
        self.me = lax.axis_index("ctx")
        self.y = lax.axis_index("tp")
        self.a, self.b, self.c = self.me // 4, (self.me // 2) % 2, self.me % 2
        a, b, c, y = self.a, self.b, self.c, self.y
        self.device = {
            UP: (self.index(jnp.minimum(a + 1, line - 1), b, c), y),
            DOWN: (self.index(jnp.maximum(a - 1, 0), b, c), y),
            ACROSS: (self.index(a, 1 - b, c), y),
            OTHER: (self.me, 1 - y),
            CORE: (self.index(a, b, 1 - c), y),
        }

    def index(self, a, b, c):
        return a * 4 + b * 2 + c

    def far_first(self, turn):
        line = self.line
        high, low = line - 1 - turn, turn
        high = jnp.where(high <= self.a, high - 1, high)
        low = jnp.where(low >= self.a, low + 1, low)
        other = jnp.where(self.a < line // 2, high, low)
        return jnp.where(turn == line - 1, self.a, other)

    def greet(self):
        barrier = pltpu.get_barrier_semaphore()
        count = 4 * self.line

        def signal(step, carry):
            pl.semaphore_signal(
                barrier, inc=1, device_id=(lax.rem(self.me + step, count), self.y), device_id_type=MESH
            )
            return carry

        lax.fori_loop(1, count, signal, 0)
        pl.semaphore_signal(barrier, inc=1, device_id=self.device[OTHER], device_id_type=MESH)
        pl.semaphore_wait(barrier, count)


class Exchange:
    def __init__(self, place, chunk, received, send, receive, own):
        self.place, self.chunk, self.received = place, chunk, received
        self.send, self.receive, self.own = send, receive, own
        self.count = 4 * place.line

    def copy(self, step, n, came):
        place, count = self.place, self.count
        to = lax.rem(place.me + step, count)
        owner = lax.rem(place.me + count - step, count) if came else place.me
        return remote(
            self.chunk(n, to), self.received(n, owner), self.send.at[n, step], self.receive.at[n, step],
            (to, place.y),
        )

    def kept(self, n):
        me = self.place.me
        return pltpu.make_async_copy(self.chunk(n, me), self.received(n, me), self.own.at[n])

    def start(self, pieces):
        for n in pieces:
            self.kept(n).start()

        def one(step, carry):
            for n in pieces:
                self.copy(step, n, False).start()
            return carry

        lax.fori_loop(1, self.count, one, 0)

    def wait(self, pieces):
        def one(step, carry):
            for n in pieces:
                self.copy(step, n, True).wait()
            return carry

        lax.fori_loop(1, self.count, one, 0)
        for n in pieces:
            self.kept(n).wait()


def row_stats(ref, slot, features, piece):
    rows = ref.shape[1]
    mean = jnp.zeros((rows, 1), F32)
    for at in range(0, features, piece):
        mean += jnp.sum(ref[slot, :, at : at + piece].astype(F32), axis=1, keepdims=True)
    mean = mean / features
    spread = jnp.zeros((rows, 1), F32)
    for at in range(0, features, piece):
        center = ref[slot, :, at : at + piece].astype(F32) - mean
        spread += jnp.sum(center * center, axis=1, keepdims=True)
    return mean, lax.rsqrt(spread / features + EPS)


def gelu_parts(value):
    inner = math.sqrt(2.0 / math.pi) * (value + 0.044715 * value * value * value)
    return jnp.tanh(inner)


def seen(start_key, start_query, keys, queries):
    key = start_key + lax.broadcasted_iota(jnp.int32, (keys, queries), 0)
    return key <= start_query + lax.broadcasted_iota(jnp.int32, (keys, queries), 1)


def collect_kernel(
    line, order_ref, inverse_ref, tok_ref, cot_ref, qkv_ref, out_ref, up_ref, down_ref, gain_ref,
    shift_ref, batt_ref, bup_ref, angle_ref,
    x_ref, g_ref, watt_ref, wup_ref, wdown_ref, normed_ref, qkvs_ref, lse_ref, attt_ref, att_ref,
    act_ref, upward_ref, gatt_ref,
    packed, watt_s, wup_s, normed_s, mixed_s, buf, k_s, vt_s, st, att_s,
    send, receive, own_sem, wsend, wreceive, wlocal, buf_sem, out_sem,
):
    place = Place(line)
    a, b, c, y = place.a, place.b, place.c, place.y
    sources, targets = (tok_ref, cot_ref), (x_ref, g_ref)
    rows, features = tok_ref.shape
    half = rows // 2
    weight_rows = up_ref.shape[0]
    tokens = x_ref.shape[0]
    hidden = wup_ref.shape[1]
    width = watt_s.shape[1] // 4
    block = 2 * rows
    blocks = tokens // block
    piece = 512
    place.greet()

    def copy(t, kind, owner, part, own=False):
        target = targets[t].at[at_rows(owner * rows + part * half, half)]
        source = sources[t].at[at_rows(part * half, half)] if own else target
        return remote(
            source, target, send.at[t, kind, owner, part], receive.at[t, owner, part], place.device[kind]
        )

    def landed(t, owner, part):
        copy(t, CORE, owner, part).wait_recv()

    def along(t, distance):
        for sign in (0,) if distance == 0 else (1, -1):
            at = a + sign * distance

            def pass_on(sign=sign, at=at):
                owner = place.index(at, b, c)
                own = distance == 0
                if not own:
                    landed(t, owner, y)
                if sign <= 0:
                    pl.when(a < line - 1)(lambda: copy(t, UP, owner, y, own).start())
                if sign >= 0:
                    pl.when(a > 0)(lambda: copy(t, DOWN, owner, y, own).start())
                copy(t, ACROSS, owner, y, own).start()
                if not own:
                    copy(t, OTHER, owner, y).start()
                copy(t, CORE, owner, y, own).start()
                if own:
                    copy(t, CORE, owner, 1 - y, own).start()

            if distance == 0:
                pass_on()
            else:
                pl.when((at >= 0) & (at < line))(pass_on)

    def beside(t, distance):
        for sign in (0,) if distance == 0 else (1, -1):
            at = a + sign * distance

            def pass_on(at=at):
                owner = place.index(at, 1 - b, c)
                landed(t, owner, y)
                copy(t, OTHER, owner, y).start()
                copy(t, CORE, owner, y).start()

            pl.when((at >= 0) & (at < line))(pass_on)

    def from_other(t):
        for distance in range(line):
            for column in (b, 1 - b):
                for sign in (0,) if distance == 0 else (1, -1):
                    at = a + sign * distance

                    def pass_on(at=at, column=column):
                        owner = place.index(at, column, c)
                        landed(t, owner, 1 - y)
                        copy(t, CORE, owner, 1 - y).start()

                    if distance == 0 and column is b:
                        continue
                    pl.when((at >= 0) & (at < line))(pass_on)

    def own_copy(t):
        return pltpu.make_async_copy(
            sources[t], targets[t].at[at_rows(place.me * rows, rows)], own_sem.at[t]
        )

    def complete(t):
        def came(chip, carry):
            for part in range(2):
                landed(t, chip * 2 + (1 - c), part)
            return carry

        lax.fori_loop(0, 2 * line, came, 0)
        own_copy(t).wait()

    def chunk(n, to):
        if n == 0:
            return packed.at[to]
        return (up_ref, down_ref)[n - 1].at[:, at_rows(to * hidden, hidden)]

    def received(n, owner):
        return (watt_s, wup_s, wdown_ref)[n].at[at_rows(owner * weight_rows, weight_rows)]

    weights = Exchange(place, chunk, received, wsend, wreceive, wlocal)

    def spread_out(t):
        for distance in range(1, line):
            along(t, distance)
            beside(t, distance - 1)
        beside(t, line - 1)

    own_copy(0).start()
    own_copy(1).start()
    along(0, 0)
    for owner in range(4 * line):
        columns = pl.ds(owner * width, width)
        packed[owner, :, :] = jnp.concatenate(
            [qkv_ref[:, kind, columns] for kind in range(3)] + [out_ref[:, columns]], axis=1
        )
    spread_out(0)
    along(1, 0)
    weights.start((0,))
    spread_out(1)
    weights.start((1, 2))
    from_other(0)
    complete(0)
    weights.wait((0,))

    def rows_in(source, at, slot):
        return pltpu.make_async_copy(
            source.at[at_rows(at * block, block)], buf.at[slot], buf_sem.at[slot]
        )

    def normed_out(at):
        here = at_rows(at * block, block)
        return pltpu.make_async_copy(normed_s.at[here], normed_ref.at[here], out_sem)

    def step_rows(source, at):
        slot = lax.rem(at, 2)
        rows_in(source, at, slot).wait()

        @pl.when(at + 1 < blocks)
        def _():
            rows_in(source, at + 1, 1 - slot).start()

        return slot, at_rows(at * block, block)

    quarter = tokens // inverse_ref.shape[0]
    quarters = block // quarter
    rows_in(x_ref, 0, 0).start()

    def project(at, carry):
        slot, here = step_rows(x_ref, at)
        mean, inv_std = row_stats(buf, slot, features, piece)
        for start in range(0, features, piece):
            part = pl.ds(start, piece)
            unit = (buf[slot, :, start : start + piece].astype(F32) - mean) * inv_std
            normed_s[here, part] = (unit * gain_ref[:, part] + shift_ref[:, part]).astype(BF)
        mixed = mm(normed_s[here, :], watt_s[...]) + batt_ref[...]
        mixed_s[pl.ds(at * quarters, quarters)] = mixed.reshape(quarters, quarter, 4 * width)
        return carry

    lax.fori_loop(0, blocks, project, 0)
    whole_normed = pltpu.make_async_copy(normed_s, normed_ref, out_sem)
    whole_normed.start()

    wide = 2 * block
    scale = 1.0 / math.sqrt(HEAD)

    def prepare(at, carry):
        here = at_rows(at * block, block)
        mixed = jnp.concatenate(
            [mixed_s[inverse_ref[at * quarters + n]] for n in range(quarters)], axis=0
        )
        cosine, sine = angle_ref[here, : ROT // 2], angle_ref[here, ROT // 2 :]
        query = turned(mixed[:, :HEAD], cosine, sine).astype(BF) * jnp.asarray(scale, BF)
        key = turned(mixed[:, HEAD : 2 * HEAD], cosine, sine)
        value = mixed[:, 2 * HEAD : 3 * HEAD]
        k_s[here, :] = key.astype(BF)
        vt_s[:, here] = jnp.concatenate([value, value], axis=1).T[:HEAD].astype(BF)
        qkvs_ref[here, :] = jnp.concatenate(
            [query, key.astype(BF), value.astype(BF), jnp.zeros_like(query)], axis=1
        )
        return carry

    lax.fori_loop(0, blocks, prepare, 0)

    def forward(at, carry):
        here = at_rows(at * block, block)
        query = qkvs_ref[here, :][:, :HEAD]

        def scored(place_at, top, masked):
            there = at_rows(place_at * wide, wide)
            scores = mm(k_s[there, :], query, NT)
            if masked:
                scores = jnp.where(seen(place_at * wide, at * block, wide, block), scores, NEG)
            st[there, :] = scores
            return jnp.maximum(top, jnp.max(scores.reshape(wide // 8, 8, block), axis=0))

        last = at // 2
        top = lax.fori_loop(
            0, last, lambda n, top: scored(n, top, False), jnp.full((8, block), NEG, F32)
        )
        top = jnp.max(scored(last, top, True), axis=0, keepdims=True)

        def weighed(place_at, state):
            total, summed = state
            there = at_rows(place_at * wide, wide)
            expo = jnp.exp(st[there, :] - top)
            total = total + jnp.sum(expo.reshape(wide // 8, 8, block), axis=0)
            return (total, summed + mm(vt_s[:, there], expo.astype(BF)))

        total, summed = lax.fori_loop(
            0, last + 1, weighed, (jnp.zeros((8, block), F32), jnp.zeros((HEAD, block), F32))
        )
        total = jnp.sum(total, axis=0, keepdims=True)
        attended = summed * (1.0 / total)
        lse_ref[:, here] = jnp.broadcast_to(top + jnp.log(total), (8, block))
        attt_ref[:, here] = attended
        both = jnp.concatenate([attended, attended], axis=0).T.astype(BF)
        att_s[pl.ds(at * quarters, quarters)] = both.reshape(quarters, quarter, 2 * HEAD)
        return carry

    lax.fori_loop(0, blocks, forward, 0)

    def unplace(at, carry):
        attended = att_s[order_ref[at]][:, HEAD:]
        att_ref[at_rows(at * quarter, quarter), :] = jnp.concatenate(
            [jnp.zeros((quarter, 3 * HEAD), BF), attended], axis=1
        )
        return carry

    lax.fori_loop(0, tokens // quarter, unplace, 0)
    from_other(1)
    complete(1)
    rows_in(g_ref, 0, 0).start()

    def grad_in(at, carry):
        slot, here = step_rows(g_ref, at)
        grad = mm(buf[slot], watt_s[...]).astype(BF)
        gatt_ref[pl.ds(at * quarters, quarters)] = grad.reshape(quarters, quarter, 4 * width)
        return carry

    lax.fori_loop(0, blocks, grad_in, 0)
    weights.wait((1,))

    def feed(at, carry):
        here = at_rows(at * block, block)
        upward = mm(normed_s[here, :], wup_s[...]) + bup_ref[...]
        upward_ref[here, :] = upward
        act_ref[here, :] = (0.5 * upward * (1.0 + gelu_parts(upward))).astype(BF)
        return carry

    lax.fori_loop(0, blocks, feed, 0)
    watt_ref[...] = watt_s[...]
    wup_ref[...] = wup_s[...]
    for t in range(2):

        def left(at, carry, t=t):
            owner, beyond = place.index(at, b, c), place.index(at, 1 - b, c)
            pl.when((at <= a) & (a < line - 1))(lambda: copy(t, UP, owner, y).wait_send())
            pl.when((at >= a) & (a > 0))(lambda: copy(t, DOWN, owner, y).wait_send())
            copy(t, ACROSS, owner, y).wait_send()
            pl.when(at != a)(lambda: copy(t, OTHER, owner, y).wait_send())
            copy(t, OTHER, beyond, y).wait_send()
            for part in range(2):
                copy(t, CORE, owner, part).wait_send()
                copy(t, CORE, beyond, part).wait_send()
            return carry

        lax.fori_loop(0, line, left, 0)
    whole_normed.wait()
    weights.wait((2,))


def collect(
    order, inverse, tokens, cotangent, qkv_weight, out_weight, fc1_weight, fc2_weight, gain, shift,
    bias_att, bias_up, angles,
):
    rows, features = tokens.shape
    weight_rows = fc1_weight.shape[0]
    count = lax.axis_size("ctx")
    line, width, hidden = count // 4, qkv_weight.shape[2] // count, fc1_weight.shape[1] // count
    total, depth = count * rows, count * weight_rows
    halves = order.shape[0]
    hbm, vmem = pl.BlockSpec(memory_space=pl.ANY), pl.BlockSpec(memory_space=pltpu.VMEM)
    smem = pl.BlockSpec(memory_space=pltpu.SMEM)
    dma = pltpu.SemaphoreType.DMA
    shape = jax.ShapeDtypeStruct
    return pl.pallas_call(
        functools.partial(collect_kernel, line),
        out_shape=[
            shape((total, features), BF),
            shape((total, features), BF),
            shape((depth, 4 * width), BF),
            shape((depth, hidden), BF),
            shape((depth, hidden), BF),
            shape((total, features), BF),
            shape((total, 4 * width), BF),
            shape((8, total), F32),
            shape((width, total), F32),
            shape((total, 4 * width), BF),
            shape((total, hidden), BF),
            shape((total, hidden), F32),
            shape((halves, total // halves, 4 * width), BF),
        ],
        in_specs=[smem, smem, hbm, hbm, vmem, vmem, hbm, hbm] + [vmem] * 5,
        out_specs=[hbm, hbm, vmem, vmem, hbm, hbm] + [vmem] * 7,
        scratch_shapes=[
            pltpu.VMEM((count, weight_rows, 4 * width), BF),
            pltpu.VMEM((depth, 4 * width), BF),
            pltpu.VMEM((depth, hidden), BF),
            pltpu.VMEM((total, features), BF),
            pltpu.VMEM((halves, total // halves, 4 * width), F32),
            pltpu.VMEM((2, 2 * rows, features), BF),
            pltpu.VMEM((total, width), BF),
            pltpu.VMEM((width, total), BF),
            pltpu.VMEM((total, 2 * rows), F32),
            pltpu.VMEM((halves, total // halves, 2 * width), BF),
            dma((2, 5, count, 2)),
            dma((2, count, 2)),
            dma((2,)),
            dma((3, count)),
            dma((3, count)),
            dma((3,)),
            dma((2,)),
            dma,
        ],
        compiler_params=pltpu.CompilerParams(
            collective_id=1, has_side_effects=True, vmem_limit_bytes=56 * 1024 * 1024
        ),
    )(
        order, inverse, tokens, cotangent, qkv_weight, out_weight, fc1_weight, fc2_weight, gain, shift,
        bias_att, bias_up, angles,
    )


def spread_kernel(
    line, order_ref, inverse_ref, att_ref, act_ref, upward_ref, gatt_ref, qkvs_ref, lse_ref, attt_ref,
    watt_ref, wup_ref, wdown_ref, angle_ref, normed_ref, g_ref, x_ref,
    sum_ref, gsum_ref, ratt_ref, rup_ref, rdown_ref, rbias_ref, norms_ref, total_ref,
    fresh, own, from_core, from_other, from_across, from_line, done, turned_s, dsend, cols, buf,
    gain_s, shift_s, nsend, nfrom, nline, bias_s, gmix_s, gup_s, kt_s, dkv_s, gm_s,
    cols_sem, buf_sem, csend, creceive, ysend, yreceive, xsend, xreceive, zsend, zreceive, fsend,
    freceive, wsend, wreceive, wlocal, nsend_sem, nreceive, lsend, lreceive,
):
    place = Place(line)
    a, b, c, y = place.a, place.b, place.c, place.y
    sums = (sum_ref, gsum_ref)
    rows, features = own.shape[2:]
    half = rows // 2
    chips = 2 * line
    tokens = att_ref.shape[0]
    block = 2 * rows
    blocks = tokens // block
    weight_rows = dsend.shape[1] // (2 * chips)
    pair = 2 * weight_rows
    piece = 512
    place.greet()
    mine, theirs = at_rows(y * half, half), at_rows((1 - y) * half, half)
    both, sibling = at_rows(c * rows, rows), at_rows((1 - c) * rows, rows)

    def chunk(n, to):
        if n == 3:
            return bias_s
        return dsend.at[n, at_rows(to * weight_rows, weight_rows)]

    def received(n, owner):
        return (ratt_ref, rup_ref, rdown_ref, rbias_ref)[n].at[owner]

    weights = Exchange(place, chunk, received, wsend, wreceive, wlocal)

    def order(turn):
        at = place.far_first(turn // 2)
        return at, at * 2 + jnp.where(lax.rem(turn, 2) == 0, 1 - b, b)

    def to_core(t, turn):
        return remote(
            fresh.at[lax.rem(turn, 2), sibling], from_core.at[t, order(turn)[1]], csend.at[t, turn],
            creceive.at[t, order(turn)[1]], place.device[CORE],
        )

    def to_other(t, chip):
        return remote(
            own.at[t, chip, theirs], from_other.at[t, chip], ysend.at[t, chip], yreceive.at[t, chip],
            place.device[OTHER],
        )

    def to_across(t, at):
        return remote(
            own.at[t, at * 2 + 1 - b, mine], from_across.at[t, at], xsend.at[t, at], xreceive.at[t, at],
            place.device[ACROSS],
        )

    def to_up(t, at):
        return remote(
            own.at[t, at * 2 + b, mine], from_line.at[t, at], zsend.at[t, at], zreceive.at[t, at],
            place.device[UP],
        )

    def to_down(t, at, last):
        slot = line if last else at
        return remote(
            own.at[t, at * 2 + b, mine], from_line.at[t, slot], zsend.at[t, at], zreceive.at[t, slot],
            place.device[DOWN],
        )

    def final(t, part):
        return remote(
            done.at[t, part], done.at[t, part], fsend.at[t], freceive.at[t], place.device[OTHER]
        )

    def add(t, chip, part, other):
        own[t, chip, part, :] = (own[t, chip, part, :].astype(F32) + other.astype(F32)).astype(BF)

    def columns_in(source, n, chip, slot):
        return pltpu.make_async_copy(
            source.at[:, at_rows(chip * pair, pair)], cols.at[n, slot], cols_sem.at[n, slot]
        )

    def rows_in(source, at, slot):
        return pltpu.make_async_copy(
            source.at[at_rows(at * block, block)], buf.at[slot], buf_sem.at[slot]
        )

    rows_in(g_ref, 0, 0).start()
    for n, source in enumerate((normed_ref, g_ref)):
        columns_in(source, n, 0, 0).start()

    def product(t, turn):
        _, chip = order(turn)
        here = at_rows(chip * block, block)
        fresh_at = lax.rem(turn, 2)
        left = ((att_ref, act_ref), (gmix_s, gup_s))[t]
        right = ((watt_ref, wdown_ref), (watt_ref, wup_ref))[t]
        first, second = left[0][here, :], left[1][here, :]
        if t == 1:
            slot = lax.rem(turn, 2)
            rows_in(x_ref, chip, slot).wait()

            @pl.when(turn + 1 < chips)
            def _():
                rows_in(x_ref, order(turn + 1)[1], 1 - slot).start()

            mean, inv_std = row_stats(buf, slot, features, piece)
        for start in range(0, features, piece):
            part = pl.ds(start, piece)
            value = mm(first, right[0][part, :], NT) + mm(second, right[1][part, :], NT)
            fresh[fresh_at, :, part] = value.astype(BF)
            if t == 1:
                unit = (buf[slot, :, start : start + piece].astype(F32) - mean) * inv_std
                shift_s[:, part] += jnp.sum(value.reshape(block // 8, 8, piece), axis=0)
                gain_s[:, part] += jnp.sum((unit * value).reshape(block // 8, 8, piece), axis=0)
        to_core(t, turn).start()

    def stage_core(t, turn):
        _, chip = order(turn)
        to_core(t, turn).wait_recv()
        own[t, chip, :, :] = (
            fresh[lax.rem(turn, 2), both, :].astype(F32) + from_core[t, chip].astype(F32)
        ).astype(BF)
        to_other(t, chip).start()
        to_core(t, turn).wait_send()

    def stage_other(t, nth):
        at = place.far_first(nth)
        chip = at * 2 + 1 - b
        to_other(t, chip).wait_recv()
        add(t, chip, mine, from_other[t, chip])
        to_across(t, at).start()

    def stage_line(t, nth):
        at = place.far_first(nth)
        chip = at * 2 + b
        to_other(t, chip).wait_recv()
        to_across(t, at).wait_recv()
        add(t, chip, mine, from_other[t, chip].astype(F32) + from_across[t, at].astype(F32))

        def down():
            @pl.when(a < line - 1)
            def _():
                to_down(t, at, False).wait_recv()
                add(t, chip, mine, from_line[t, at])

            pl.when(at == a - 1)(lambda: to_down(t, at, True).start())
            pl.when(at < a - 1)(lambda: to_down(t, at, False).start())

        def up():
            @pl.when(a > 0)
            def _():
                to_up(t, at).wait_recv()
                add(t, chip, mine, from_line[t, at])

            to_up(t, at).start()

        if nth < line - 1:
            pl.when(at < a)(down)
            pl.when(at > a)(up)
            return

        @pl.when(a < line - 1)
        def _():
            to_down(t, at, True).wait_recv()
            add(t, chip, mine, from_line[t, line])

        @pl.when(a > 0)
        def _():
            to_up(t, at).wait_recv()
            add(t, chip, mine, from_line[t, at])

        done[t, mine, :] = own[t, chip, mine, :]
        final(t, mine).start()

    def stages(t):
        steps = [functools.partial(stage_other, t, 0)]
        for nth in range(1, line):
            steps.append(functools.partial(stage_other, t, nth))
            steps.append(functools.partial(stage_line, t, nth - 1))
        steps.append(functools.partial(stage_line, t, line - 1))
        return steps

    def norm_copy(step):
        kind = (CORE, OTHER, ACROSS)[step]
        return remote(
            nsend.at[step], nfrom.at[step], nsend_sem.at[step], nreceive.at[step], place.device[kind]
        )

    def norm_line(other, came):
        return remote(
            nsend.at[3], nline.at[other if came else a], lsend.at[other],
            lreceive.at[other if came else a], (place.index(other, b, c), y),
        )

    product(0, 0)

    def first_sum(turn, carry):
        product(0, turn)
        stage_core(0, turn - 1)
        return carry

    lax.fori_loop(1, chips, first_sum, 0)
    stage_core(0, chips - 1)
    pending = stages(0)

    def feed_back(at, carry):
        slot = lax.rem(at, 2)
        rows_in(g_ref, at, slot).wait()

        @pl.when(at + 1 < blocks)
        def _():
            rows_in(g_ref, at + 1, 1 - slot).start()

        here = at_rows(at * block, block)
        upward = upward_ref[here, :]
        tanh = gelu_parts(upward)
        slope = 0.5 * (1.0 + tanh) + 0.5 * upward * (1.0 - tanh * tanh) * (
            math.sqrt(2.0 / math.pi) * (1.0 + 3 * 0.044715 * upward * upward)
        )
        gup_s[here, :] = (mm(buf[slot], wdown_ref[...]) * slope).astype(BF)
        return carry

    lax.fori_loop(0, blocks // 2, feed_back, 0)
    pending.pop(0)()
    lax.fori_loop(blocks // 2, blocks, feed_back, 0)
    rows_in(x_ref, order(0)[1], 0).start()

    def turn_over(pieces):
        def one(at, carry):
            here = at_rows(at * 256, 256)
            for n, source in pieces:
                turned_s[n, :, here] = source[here, :].T
            return carry

        lax.fori_loop(0, tokens // 256, one, 0)

    turn_over(((1, gup_s), (2, att_ref), (3, act_ref)))
    ones = jnp.ones((8, tokens), BF)

    def gradients(chip, carry):
        slot = lax.rem(chip, 2)
        for n, source in enumerate((normed_ref, g_ref)):
            columns_in(source, n, chip, slot).wait()

            @pl.when(chip + 1 < chips)
            def _(n=n, source=source):
                columns_in(source, n, chip + 1, 1 - slot).start()

        here = at_rows(chip * pair, pair)
        by_normed, by_grad = cols[0, slot], cols[1, slot]
        dsend[0, here, :] = mm(turned_s[2], by_grad).T.astype(BF)
        dsend[1, here, :] = mm(turned_s[1], by_normed).T.astype(BF)
        dsend[2, here, :] = mm(turned_s[3], by_grad).T.astype(BF)
        total_ref[:, here] = mm(ones, by_grad)
        return carry

    lax.fori_loop(0, chips // 2, gradients, 0)
    pending.pop(0)()
    lax.fori_loop(chips // 2, chips, gradients, 0)
    weights.start((1, 2))
    columns_in(normed_ref, 0, 0, 0).start()
    pending.pop(0)()

    quarter = tokens // inverse_ref.shape[0]
    quarters = block // quarter
    wide = 2 * block
    scale = 1.0 / math.sqrt(HEAD)

    def prepare(at, carry):
        here = at_rows(at * block, block)
        key = qkvs_ref[here, :][:, : 2 * HEAD].astype(F32)
        kt_s[:, here] = key.T[HEAD:].astype(BF)
        dkv_s[here, :] = jnp.zeros((block, 2 * HEAD), F32)
        return carry

    lax.fori_loop(0, blocks, prepare, 0)

    def backward(at, carry):
        here = at_rows(at * block, block)
        query = qkvs_ref[here, :][:, :HEAD]
        grad = jnp.concatenate(
            [gatt_ref[inverse_ref[at * quarters + n]] for n in range(quarters)], axis=0
        )
        left = lax.broadcasted_iota(jnp.int32, (block, 2 * HEAD), 1) < HEAD
        grad_wide = grad[:, 2 * HEAD :].astype(F32)
        grad_right = jnp.where(left, 0.0, grad_wide).astype(BF)
        query_left = jnp.concatenate([query, jnp.zeros_like(query)], axis=1)
        grad = grad[:, 3 * HEAD :]
        delta = jnp.sum(grad_wide.T[HEAD:] * attt_ref[:, here], axis=0, keepdims=True)
        lse = lse_ref[0:1, here]

        def back(place_at, query_grad, masked):
            there = at_rows(place_at * wide, wide)
            keyvalue = qkvs_ref[there, :]
            scores = mm(keyvalue[:, HEAD : 2 * HEAD], query, NT)
            if masked:
                scores = jnp.where(seen(place_at * wide, at * block, wide, block), scores, NEG)
            prob = jnp.exp(scores - lse)
            dprob = mm(keyvalue[:, 2 * HEAD : 3 * HEAD], grad, NT)
            dscore = (prob * (dprob - delta)).astype(BF)
            dkv_s[there, :] += mm(dscore, query_left) + mm(prob.astype(BF), grad_right)
            return query_grad + mm(kt_s[:, there], dscore)

        last = at // 2
        query_grad = lax.fori_loop(
            0, last, lambda n, total: back(n, total, False), jnp.zeros((HEAD, block), F32)
        )
        query_grad = back(last, query_grad, True)
        query_grad = jnp.concatenate([query_grad, query_grad], axis=0).T[:, :HEAD]
        query_grad = turned(
            query_grad * scale, angle_ref[here, : ROT // 2], -angle_ref[here, ROT // 2 :]
        ).astype(BF)
        gm_s[pl.ds(at * quarters, quarters), :, pl.ds(0, HEAD)] = query_grad.reshape(
            quarters, quarter, HEAD
        )
        return carry

    done_blocks = 0
    for upto in (blocks // 2, blocks * 3 // 4, blocks * 7 // 8, blocks):
        lax.fori_loop(done_blocks, upto, backward, 0)
        done_blocks = upto
        pending.pop(0)()

    def finish_keys(at, carry):
        here = at_rows(at * block, block)
        keyvalue = jnp.concatenate(
            [
                turned(
                    dkv_s[here, :][:, :HEAD], angle_ref[here, : ROT // 2], -angle_ref[here, ROT // 2 :]
                ).astype(BF),
                dkv_s[here, :][:, HEAD:].astype(BF),
            ],
            axis=1,
        )
        gm_s[pl.ds(at * quarters, quarters), :, pl.ds(HEAD, 2 * HEAD)] = keyvalue.reshape(
            quarters, quarter, 2 * HEAD
        )
        return carry

    lax.fori_loop(0, blocks, finish_keys, 0)

    def unplace(at, carry):
        gmix_s[at_rows(at * quarter, quarter), :] = jnp.concatenate(
            [gm_s[order_ref[at]], jnp.zeros((quarter, HEAD), BF)], axis=1
        )
        return carry

    lax.fori_loop(0, tokens // quarter, unplace, 0)
    turn_over(((0, gmix_s),))
    for n, source in enumerate((gmix_s, gup_s)):
        columns = source.shape[1]

        def tally(at, total, source=source, columns=columns):
            return total + jnp.sum(
                source[at_rows(at * 256, 256), :].astype(F32).reshape(32, 8, columns), axis=0
            )

        total = lax.fori_loop(0, tokens // 256, tally, jnp.zeros((8, columns), F32))
        total = jnp.sum(total, axis=0, keepdims=True)
        for at in range(columns // 128):
            bias_s[pl.ds(n * 2 + at, 1), :] = total[:, at * 128 : (at + 1) * 128]
    bias_s[pl.ds(4, 4), :] = jnp.zeros((4, 128), F32)

    gain_s[...] = jnp.zeros_like(gain_s)
    shift_s[...] = jnp.zeros_like(shift_s)

    def gradients_att(chip):
        slot = lax.rem(chip, 2)
        columns_in(normed_ref, 0, chip, slot).wait()

        @pl.when(chip + 1 < chips)
        def _():
            columns_in(normed_ref, 0, chip + 1, 1 - slot).start()

        here = at_rows(chip * pair, pair)
        more = mm(turned_s[0], cols[0, slot]).T
        dsend[0, here, :] = (dsend[0, here, :].astype(F32) + more).astype(BF)

    product(1, 0)

    def second_sum(turn, carry):
        product(1, turn)
        stage_core(1, turn - 1)
        gradients_att(turn - 1)
        return carry

    lax.fori_loop(1, chips, second_sum, 0)
    stage_core(1, chips - 1)
    gradients_att(chips - 1)
    weights.start((0, 3))
    for step in pending:
        step()
    for n, source in enumerate((gain_s, shift_s)):
        total = jnp.sum(source[...], axis=0, keepdims=True)
        span = features // 4
        for at in range(4):
            nsend[0, pl.ds(n * 4 + at, 1), :] = total[:, at * span : (at + 1) * span]
    norm_copy(0).start()
    pending = stages(1)
    pending.pop(0)()
    norm_copy(0).wait_recv()
    nsend[1] = nsend[0] + nfrom[0]
    norm_copy(1).start()
    pending.pop(0)()
    pending.pop(0)()
    norm_copy(1).wait_recv()
    nsend[2] = nsend[1] + nfrom[1]
    norm_copy(2).start()
    pending.pop(0)()
    pending.pop(0)()
    norm_copy(2).wait_recv()
    nsend[3] = nsend[2] + nfrom[2]
    nline[a] = nsend[3]
    for other in range(line):
        pl.when(a != other)(lambda other=other: norm_line(other, False).start())
    for step in pending:
        step()
    for other in range(line):
        pl.when(a != other)(lambda other=other: norm_line(other, True).wait_recv())
    total = nline[0]
    for other in range(1, line):
        total += nline[other]
    norms_ref[...] = total

    for step in range(3):
        norm_copy(step).wait_send()
    for other in range(line):
        pl.when(a != other)(lambda other=other: norm_line(other, False).wait_send())
    for t in range(2):
        final(t, theirs).wait_recv()
        final(t, mine).wait_send()
        sums[t][...] = done[t]

        def left(at, carry, t=t):
            to_other(t, at * 2).wait_send()
            to_other(t, at * 2 + 1).wait_send()
            to_across(t, at).wait_send()
            pl.when(at != a)(lambda: to_up(t, at).wait_send())
            return carry

        lax.fori_loop(0, line, left, 0)
    weights.wait((0, 1, 2, 3))


def spread(
    order, inverse, attended, activated, upward, grad_att, qkvs, lse, attended_t, w_att, w_up, w_down,
    angles, normed, g_all, x_all,
):
    count = lax.axis_size("ctx")
    line = count // 4
    tokens, features = x_all.shape
    rows = tokens // count
    half = rows // 2
    chips = 2 * line
    weight_rows = w_att.shape[0] // count
    wide, hidden = w_att.shape[1], w_up.shape[1]
    hbm, vmem = pl.BlockSpec(memory_space=pl.ANY), pl.BlockSpec(memory_space=pltpu.VMEM)
    smem = pl.BlockSpec(memory_space=pltpu.SMEM)
    dma = pltpu.SemaphoreType.DMA
    own = jax.ShapeDtypeStruct((rows, features), BF)
    back = [
        jax.ShapeDtypeStruct((count, weight_rows, columns), BF) for columns in (wide, hidden, hidden)
    ]
    return pl.pallas_call(
        functools.partial(spread_kernel, line),
        out_shape=[own, own]
        + back
        + [
            jax.ShapeDtypeStruct((count, 8, 128), F32),
            jax.ShapeDtypeStruct((8, features // 4), F32),
            jax.ShapeDtypeStruct((8, features), F32),
        ],
        in_specs=[smem, smem] + [vmem] * 11 + [hbm] * 3,
        out_specs=[vmem, vmem, hbm, hbm, hbm, hbm, vmem, vmem],
        scratch_shapes=[
            pltpu.VMEM((2, 2 * rows, features), BF),
            pltpu.VMEM((2, chips, rows, features), BF),
            pltpu.VMEM((2, chips, rows, features), BF),
            pltpu.VMEM((2, chips, half, features), BF),
            pltpu.VMEM((2, line, half, features), BF),
            pltpu.VMEM((2, line + 1, half, features), BF),
            pltpu.VMEM((2, rows, features), BF),
            pltpu.VMEM((4, wide, tokens), BF),
            pltpu.VMEM((3, count * weight_rows, wide), BF),
            pltpu.VMEM((2, 2, tokens, 2 * weight_rows), BF),
            pltpu.VMEM((2, 2 * rows, features), BF),
            pltpu.VMEM((8, features), F32),
            pltpu.VMEM((8, features), F32),
            pltpu.VMEM((4, 8, features // 4), F32),
            pltpu.VMEM((3, 8, features // 4), F32),
            pltpu.VMEM((line, 8, features // 4), F32),
            pltpu.VMEM((8, 128), F32),
            pltpu.VMEM((tokens, wide), BF),
            pltpu.VMEM((tokens, hidden), BF),
            pltpu.VMEM((HEAD, tokens), BF),
            pltpu.VMEM((tokens, 2 * HEAD), F32),
            pltpu.VMEM((order.shape[0], tokens // order.shape[0], 3 * HEAD), BF),
            dma((2, 2)),
            dma((2,)),
            dma((2, chips)),
            dma((2, chips)),
            dma((2, chips)),
            dma((2, chips)),
            dma((2, line)),
            dma((2, line)),
            dma((2, line)),
            dma((2, line + 1)),
            dma((2,)),
            dma((2,)),
            dma((4, count)),
            dma((4, count)),
            dma((4,)),
            dma((3,)),
            dma((3,)),
            dma((line,)),
            dma((line,)),
        ],
        compiler_params=pltpu.CompilerParams(
            collective_id=2, has_side_effects=True, vmem_limit_bytes=63 * 1024 * 1024
        ),
    )(
        order, inverse, attended, activated, upward, grad_att, qkvs, lse, attended_t, w_att, w_up,
        w_down, angles, normed, g_all, x_all,
    )


def finish_kernel(
    tok_ref, cot_ref, gain_ref, bias_ref, branch_ref, normed_ref, datt_ref, dup_ref, ddown_ref,
    sums_ref, norms_ref, total_ref,
    out_ref, grad_ref, qkv_ref, wout_ref, up_ref, down_ref, qkvb_ref, upb_ref, gsum_ref, ssum_ref,
    bsum_ref,
):
    inputs = tok_ref[...].astype(F32)
    center = inputs - jnp.mean(inputs, axis=-1, keepdims=True)
    inv_std = lax.rsqrt(jnp.mean(center * center, axis=-1, keepdims=True) + EPS)
    unit = center * inv_std
    out_ref[...] = inputs + branch_ref[...].astype(F32) + bias_ref[...]
    grad_unit = normed_ref[...].astype(F32) * gain_ref[...]
    grad_ref[...] = cot_ref[...].astype(F32) + inv_std * (
        grad_unit
        - jnp.mean(grad_unit, axis=-1, keepdims=True)
        - unit * jnp.mean(grad_unit * unit, axis=-1, keepdims=True)
    )
    count, _, packed = datt_ref.shape
    width, hidden = packed // 4, dup_ref.shape[2]
    for owner in range(count):
        columns = pl.ds(owner * width, width)
        piece = datt_ref[owner].astype(F32)
        for kind in range(3):
            qkv_ref[:, kind, columns] = piece[:, kind * width : (kind + 1) * width]
        wout_ref[:, columns] = piece[:, 3 * width :]
        up_ref[:, pl.ds(owner * hidden, hidden)] = dup_ref[owner].astype(F32)
        down_ref[:, pl.ds(owner * hidden, hidden)] = ddown_ref[owner].astype(F32)
        for kind in range(3):
            at = kind * width
            qkvb_ref[pl.ds(kind, 1), columns] = sums_ref[owner, at // 128 : at // 128 + 1, at % 128 : at % 128 + width]
        for at in range(hidden // 128):
            upb_ref[:, pl.ds(owner * hidden + at * 128, 128)] = sums_ref[owner, 2 + at : 3 + at, :]
    wide = norms_ref.shape[1]
    for at in range(4):
        gsum_ref[:, pl.ds(at * wide, wide)] = norms_ref[at : at + 1, :]
        ssum_ref[:, pl.ds(at * wide, wide)] = norms_ref[4 + at : 5 + at, :]
    bsum_ref[...] = total_ref[0:1, :]


def finish(tokens, cotangent, gain, bias, branches, own_normed, d_att, d_up, d_down, sums, norms, total):
    count, weight_rows, packed = d_att.shape
    width, hidden = packed // 4, d_up.shape[2]
    vmem = pl.BlockSpec(memory_space=pltpu.VMEM)
    rows = jax.ShapeDtypeStruct(tokens.shape, F32)
    return pl.pallas_call(
        finish_kernel,
        out_shape=[
            rows,
            rows,
            jax.ShapeDtypeStruct((weight_rows, 3, count * width), F32),
            jax.ShapeDtypeStruct((weight_rows, count * width), F32),
            jax.ShapeDtypeStruct((weight_rows, count * hidden), F32),
            jax.ShapeDtypeStruct((weight_rows, count * hidden), F32),
            jax.ShapeDtypeStruct((3, count * width), F32),
            jax.ShapeDtypeStruct((1, count * hidden), F32),
            jax.ShapeDtypeStruct((1, tokens.shape[1]), F32),
            jax.ShapeDtypeStruct((1, tokens.shape[1]), F32),
            jax.ShapeDtypeStruct((1, tokens.shape[1]), F32),
        ],
        in_specs=[vmem] * 12,
        out_specs=[vmem] * 11,
        compiler_params=pltpu.CompilerParams(vmem_limit_bytes=50 * 1024 * 1024),
    )(
        tokens, cotangent, gain[None], bias[None], branches, own_normed, d_att, d_up, d_down, sums,
        norms, total,
    )


def gelu_tanh(value):
    return jax.nn.gelu(value, approximate=True)


def local(
    tokens, block_order, ln_gain, ln_bias, qkv_weight, qkv_bias, out_weight, fc1_weight, fc1_bias,
    fc2_weight, out_bias, cotangent,
):
    devices = lax.axis_size("ctx")
    myself = lax.axis_index("ctx")
    heads_here = qkv_weight.shape[2] // HEAD
    columns = math.gcd(devices, heads_here)
    mine = myself % columns
    width = qkv_weight.shape[2] // columns
    hidden = fc1_weight.shape[1] // columns
    bias_att = lax.dynamic_slice_in_dim(qkv_bias, mine * width, width, 1).reshape(-1)
    bias_att = jnp.concatenate([bias_att, jnp.zeros((width,), F32)])[None]
    bias_up = lax.dynamic_slice_in_dim(fc1_bias, mine * hidden, hidden, 0)[None]
    if devices == columns and columns % 8 == 0 and width == HEAD and lax.axis_size("tp") == 2:
        halves = block_order.shape[0]
        counted = jnp.arange(halves, dtype=jnp.int32)
        inverse = jnp.sum(
            jnp.where(block_order[None, :] == counted[:, None], counted[None, :], 0), axis=1
        )
        angles = tables(jnp.arange(devices * tokens.shape[0], dtype=jnp.int32), ROT)
        angles = jnp.concatenate(angles, axis=1)
        (
            x_all, g_all, w_att, w_up, w_down, normed, qkvs, lse, attended_t, attended, activated,
            upward, grad_att,
        ) = collect(
            block_order, inverse, tokens, cotangent, qkv_weight, out_weight, fc1_weight, fc2_weight,
            ln_gain[None], ln_bias[None], bias_att, bias_up, angles,
        )
        parts = spread(
            block_order, inverse, attended, activated, upward, grad_att, qkvs, lse, attended_t, w_att,
            w_up, w_down, angles, normed, g_all, x_all,
        )
    else:
        parts = by_groups(
            tokens, block_order, ln_gain, ln_bias, qkv_weight, out_weight, fc1_weight, fc2_weight,
            cotangent, bias_att, bias_up,
        )
    (
        output, input_grad, qkv_grad, out_grad, fc1_grad, fc2_grad, qkv_sums, fc1_sums, gain_sum,
        shift_sum, g_sum,
    ) = finish(tokens, cotangent, ln_gain, out_bias, *parts)
    return (
        output, input_grad, gain_sum[0], shift_sum[0], qkv_grad, qkv_sums, out_grad, fc1_grad,
        fc1_sums[0], fc2_grad, g_sum[0],
    )


def by_groups(
    tokens, block_order, ln_gain, ln_bias, qkv_weight, out_weight, fc1_weight, fc2_weight, cotangent,
    bias_att, bias_up,
):
    devices = lax.axis_size("ctx")
    myself = lax.axis_index("ctx")
    rows_here = tokens.shape[0]
    weight_rows = qkv_weight.shape[0]
    half = devices * rows_here // block_order.shape[0]
    columns = math.gcd(devices, qkv_weight.shape[2] // HEAD)
    groups = devices // columns
    width, hidden = qkv_weight.shape[2] // columns, fc1_weight.shape[1] // columns
    count = columns * rows_here
    side = [[r * columns + c for c in range(columns)] for r in range(groups)]
    across = [[r * columns + c for r in range(groups)] for c in range(columns)]

    def gathered(value, among):
        return lax.all_gather(value, "ctx", axis=0, tiled=True, axis_index_groups=among)

    def scattered(value, among):
        return lax.psum_scatter(
            value, "ctx", scatter_dimension=0, tiled=True, axis_index_groups=among
        )

    def exchanged(value):
        return lax.all_to_all(value, "ctx", split_axis=0, concat_axis=0, tiled=True)

    x_all, g_all = gathered(tokens, side), gathered(cotangent, side)
    kinds = jnp.concatenate([qkv_weight, out_weight[:, None]], axis=1)
    kinds = kinds.reshape(weight_rows, 4, columns, width).transpose(2, 0, 1, 3)
    packed = jnp.concatenate(
        [
            kinds.reshape(columns, weight_rows, 4 * width),
            fc1_weight.reshape(weight_rows, columns, hidden).transpose(1, 0, 2),
            fc2_weight.reshape(weight_rows, columns, hidden).transpose(1, 0, 2),
        ],
        axis=2,
    )
    packed = exchanged(jnp.tile(packed, (groups, 1, 1))).reshape(devices * weight_rows, -1)
    w_att, w_up, w_down = jnp.split(packed, [4 * width, 4 * width + hidden], axis=1)

    inputs = x_all.astype(F32)
    center = inputs - jnp.mean(inputs, axis=-1, keepdims=True)
    inv_std = lax.rsqrt(jnp.mean(center * center, axis=-1, keepdims=True) + EPS)
    unit = center * inv_std
    normed = (unit * ln_gain + ln_bias).astype(BF)
    upward = mm(normed, w_up) + bias_up
    activated, gelu_back = jax.vjp(gelu_tanh, upward)
    activated = activated.astype(BF)
    grad_up = gelu_back(mm(g_all, w_down))[0].astype(BF)
    places = (block_order[:, None] * half + jnp.arange(half, dtype=jnp.int32)[None, :]).reshape(-1)
    attended, grad_mixed = attention_blocks(
        lax.dynamic_slice_in_dim(places, (myself // columns) * count, count),
        places,
        mm(normed, w_att) + bias_att,
        mm(g_all, w_att),
        lambda value: gathered(value, across),
        lambda value: scattered(value, across),
    )
    out_part = (mm(attended, w_att, NT) + mm(activated, w_down, NT)).astype(BF)
    normed_wide = mm(grad_mixed, w_att, NT) + mm(grad_up, w_up, NT)
    branches, own_normed = lax.psum(
        (scattered(out_part, side), scattered(normed_wide.astype(BF), side)), "tp"
    )
    back = jnp.concatenate(
        [
            (mm(normed, grad_mixed, TN) + mm(g_all, attended, TN)).astype(BF),
            mm(normed, grad_up, TN).astype(BF),
            mm(g_all, activated, TN).astype(BF),
        ],
        axis=1,
    )
    back = exchanged(back.reshape(devices, weight_rows, -1))
    back = jnp.sum(back.reshape(groups, columns, weight_rows, -1).astype(F32), axis=0)
    sums = jnp.concatenate(
        [jnp.sum(grad_mixed.astype(F32), axis=0), jnp.sum(grad_up.astype(F32), axis=0)]
    ).reshape(-1, 128)
    sums = jnp.pad(sums, ((0, 8 - sums.shape[0]), (0, 0)))
    sums = gathered(lax.psum(sums, "ctx", axis_index_groups=across)[None], side)
    norms = jnp.stack([jnp.sum(unit * normed_wide, axis=0), jnp.sum(normed_wide, axis=0)])
    norms = lax.psum(norms, ("ctx", "tp")).reshape(8, -1)
    total = lax.psum(jnp.sum(g_all.astype(F32), axis=0), "ctx", axis_index_groups=across)[None]
    return (
        branches, own_normed, *jnp.split(back, [4 * width, 4 * width + hidden], axis=2), sums, norms,
        total,
    )


def solution(mesh):
    rows, tall = P("ctx", None), P("ctx", "tp")
    kinds, bias = P("ctx", None, "tp"), P(None, "tp")
    return jax.shard_map(
        local,
        mesh=mesh,
        in_specs=(rows, P(), P(), P(), kinds, bias, tall, tall, P("tp"), tall, P(), rows),
        out_specs=(rows, rows, P(), P(), kinds, bias, tall, tall, P("tp"), tall, P()),
        check_vma=False,
    )
```

profile of v0, /device:TPU:0, one launch (start us, length us, event | category | flops | bytes accessed | tf_op | source)
XLA Modules:
  0.0 362.7 jit_solution(11873323203926068054)
XLA Ops:
  0.6 0.0 copy-start
  0.7 0.0 copy-start.11
  0.7 1.4 select_reduce_fusion.inverse_ref
  2.0 1.3 dynamic_slice.7
  3.4 0.0 copy-done
  3.4 0.1 constant_dynamic-slice_fusion
  3.5 0.1 reshape.37
  3.5 0.6 concatenate.6
  4.1 0.5 multiply_cosine_fusion
  4.7 1.3 copy.30.angle_ref
  6.0 0.0 copy-done.11
  6.0 1.6 copy.29.qkv_ref
  7.6 156.9 %shard_map.203 = (bf16[2048,2048]{1,0:T(8,128)(2,1)}, bf16[2048,2048]{1,0:T(8,128)(2,1)}, bf16[2048,256]{1,0:T(8,128)(2,1)}, bf16[2048,256]{1,0:T(8,128)(2,1)}, ...) custom-call(s32[32]{0:T(128)} %order_ref.3, ...), custom_call_target="tpu_custom_call" | custom-call | tf_op jit(solution)/shard_map/pallas_call | solution.py:512
  164.6 0.0 copy-start.1
  164.6 0.0 copy-start.8
  164.6 0.0 copy-start.10
  164.6 178.9 %shard_map.204 = (bf16[128,2048]{1,0:T(8,128)(2,1)}, bf16[128,2048]{1,0:T(8,128)(2,1)}, bf16[16,128,256]{2,1,0:T(8,128)(2,1)}, bf16[16,128,256]{2,1,0:T(8,128)(2...) custom-call(s32[32]{0:T(128)} %order_ref.3, ...), custom_call_target="tpu_custom_call" | custom-call | tf_op jit(solution)/shard_map/pallas_call | solution.py:1025
  343.6 0.0 copy-done.1
  343.6 0.0 copy-done.8
  343.6 0.0 copy-done.10
  343.6 0.0 copy-start.2
  343.6 1.0 copy-done.2
  344.6 0.0 copy-start.3
  344.6 1.2 copy-done.3
  345.9 0.0 copy-start.4
  345.9 1.0 copy-done.4
  346.9 0.0 copy-start.5
  346.9 1.0 copy-done.5
  347.9 0.0 copy-start.6
  347.9 0.8 copy-done.6
  348.8 0.0 copy-start.7
  348.8 0.8 copy-done.7
  349.6 0.0 copy-start.9
  349.6 0.7 copy-done.9
  350.3 8.8 %shard_map.205 = (f32[128,2048]{1,0:T(8,128)}, f32[128,2048]{1,0:T(8,128)}, f32[128,3,1024]{2,1,0:T(4,128)}, f32[128,1024]{1,0:T(8,128)}, f32[128,4096]{1,0:T(8,...) custom-call(bf16[128,2048]{1,0:T(8,128)(2,1)S(1)} %copy-done.1, ...), custom_call_target="tpu_custom_call" | custom-call | tf_op jit(solution)/shard_map/pallas_call | solution.py:1132
  359.1 3.6 %copy.32 = f32[128,3,1024]{2,0,1:T(8,128)} copy(f32[128,3,1024]{2,1,0:T(4,128)} %get-tuple-element.101) | data formatting | bytes 3145728
  (3 shorter events, 0.0 us)
Async XLA Ops:
  0.6 2.7 copy-start
  0.7 5.3 %copy-start.11 = (bf16[128,3,1024]{2,0,1:T(8,128)(2,1)S(1)}, bf16[128,3,1024]{2,0,1:T(8,128)(2,1)}, u32[]{:S(2)}) copy-start(bf16[128,3,1024]{2,0,1:T(8,128)(2,1)} %param.16) | copy-start | bytes 2359300
  164.6 179.0 %copy-start.1 = (bf16[128,2048]{1,0:T(8,128)(2,1)S(1)}, bf16[128,2048]{1,0:T(8,128)(2,1)}, u32[]{:S(2)}) copy-start(bf16[128,2048]{1,0:T(8,128)(2,1)} %tok_ref.3) | copy-start | bytes 1572868
  164.6 179.0 %copy-start.8 = (f32[2048]{0:T(1024)S(1)}, f32[2048]{0:T(1024)}, u32[]{:S(2)}) copy-start(f32[2048]{0:T(1024)} %param.14) | copy-start | bytes 24580
  164.6 179.0 %copy-start.10 = (f32[2048]{0:T(1024)S(1)}, f32[2048]{0:T(1024)}, u32[]{:S(2)}) copy-start(f32[2048]{0:T(1024)} %param.22) | copy-start | bytes 24580
  343.6 1.0 copy-start.2
  344.6 1.2 copy-start.3
  345.9 1.0 copy-start.4
  346.9 1.0 copy-start.5
  347.9 0.8 copy-start.6
  348.8 0.8 copy-start.7
  349.6 0.7 copy-start.9
where the time goes:
time: 364 us; the launch traced here: 363 us
  Pallas kernels  345 us (95%)
  local copies, waits for them, and re-layouts  15.4 us (4%)
    pallas_call x1, Pallas kernels, spread(): pl.pallas_call(functools.partial(spread_kernel, line), out_shape=[own, ow...  179 us
    pallas_call x1, Pallas kernels, collect(): pl.pallas_call(functools.partial(collect_kernel, line), out_shape=[shape(...  157 us
    unnamed x26, local copies, waits for them, and re-layouts  12.1 us
    pallas_call x1, Pallas kernels, finish(): pl.pallas_call(finish_kernel, out_shape=[rows, rows, jax.ShapeDtypeStruct...  8.76 us

commit v1 on v0

--- a/solution.py
+++ b/solution.py
@@ -153,58 +153,83 @@
         pl.semaphore_wait(barrier, count)
 
 
+def flipped(value, mask, bits):
+    result = 0
+    for bit in range(bits):
+        part = (value // 2**bit) % 2
+        result = result + 2**bit * (1 - part if mask >> bit & 1 else part)
+    return result
+
+
 class Exchange:
     def __init__(self, place, chunk, received, send, receive, own):
         self.place, self.chunk, self.received = place, chunk, received
         self.send, self.receive, self.own = send, receive, own
         self.count = 4 * place.line
-
-    def copy(self, step, n, came):
-        place, count = self.place, self.count
-        to = lax.rem(place.me + step, count)
-        owner = lax.rem(place.me + count - step, count) if came else place.me
+        bits = self.count.bit_length() - 1
+        self.partners = [
+            (mask, flipped(place.me, mask, bits)) for mask in range(self.count - 1, 0, -1)
+        ]
+
+    def copy(self, partner, n, came):
+        mask, to = partner
         return remote(
-            self.chunk(n, to), self.received(n, owner), self.send.at[n, step], self.receive.at[n, step],
-            (to, place.y),
+            self.chunk(n, to), self.received(n, to if came else self.place.me), self.send.at[n, mask],
+            self.receive.at[n, mask], (to, self.place.y),
         )
 
     def kept(self, n):
         me = self.place.me
         return pltpu.make_async_copy(self.chunk(n, me), self.received(n, me), self.own.at[n])
 
-    def start(self, pieces):
+    def keep(self, pieces):
         for n in pieces:
             self.kept(n).start()
 
-        def one(step, carry):
+    def start(self, pieces, wanted=lambda at, mask: True):
+        for at, partner in enumerate(self.partners):
             for n in pieces:
-                self.copy(step, n, False).start()
-            return carry
-
-        lax.fori_loop(1, self.count, one, 0)
+                if wanted(at, partner[0]):
+                    self.copy(partner, n, False).start()
 
     def wait(self, pieces):
-        def one(step, carry):
+        for partner in self.partners:
             for n in pieces:
-                self.copy(step, n, True).wait()
-            return carry
-
-        lax.fori_loop(1, self.count, one, 0)
+                self.copy(partner, n, True).wait()
         for n in pieces:
             self.kept(n).wait()
 
 
-def row_stats(ref, slot, features, piece):
-    rows = ref.shape[1]
+def row_stats(load, rows, features, piece):
     mean = jnp.zeros((rows, 1), F32)
     for at in range(0, features, piece):
-        mean += jnp.sum(ref[slot, :, at : at + piece].astype(F32), axis=1, keepdims=True)
+        mean += jnp.sum(load(at), axis=1, keepdims=True)
     mean = mean / features
     spread = jnp.zeros((rows, 1), F32)
     for at in range(0, features, piece):
-        center = ref[slot, :, at : at + piece].astype(F32) - mean
+        center = load(at) - mean
         spread += jnp.sum(center * center, axis=1, keepdims=True)
     return mean, lax.rsqrt(spread / features + EPS)
+
+
+class Stream:
+    def __init__(self, copy, depth, total):
+        self.copy, self.depth, self.total = copy, depth, total
+
+    def prime(self):
+        for at in range(min(self.depth - 1, self.total)):
+            self.copy(at, at).start()
+
+    def step(self, at):
+        slot = lax.rem(at, self.depth)
+        self.copy(at, slot).wait()
+        later = at + self.depth - 1
+
+        @pl.when(later < self.total)
+        def _():
+            self.copy(later, lax.rem(later, self.depth)).start()
+
+        return slot
 
 
 def gelu_parts(value):
@@ -220,10 +245,11 @@
 def collect_kernel(
     line, order_ref, inverse_ref, tok_ref, cot_ref, qkv_ref, out_ref, up_ref, down_ref, gain_ref,
     shift_ref, batt_ref, bup_ref, angle_ref,
-    x_ref, g_ref, watt_ref, wup_ref, wdown_ref, normed_ref, qkvs_ref, lse_ref, attt_ref, att_ref,
-    act_ref, upward_ref, gatt_ref,
-    packed, watt_s, wup_s, normed_s, mixed_s, buf, k_s, vt_s, st, att_s,
-    send, receive, own_sem, wsend, wreceive, wlocal, buf_sem, out_sem,
+    x_out, g_out, watt_out, wup_out, wdown_ref, normed_out, qkvs_out, lse_out, attt_out, att_out,
+    act_out, upward_out, gatt_out,
+    x_ref, g_ref, watt_s, wup_s, normed_s, qkvs_ref, lse_ref, attt_ref, att_ref, act_ref, upward_ref,
+    gatt_ref, packed, mixed_s, k_s, vt_s, st, att_s,
+    send, receive, own_sem, wsend, wreceive, wlocal, out_sem,
 ):
     place = Place(line)
     a, b, c, y = place.a, place.b, place.c, place.y
@@ -232,12 +258,17 @@
     half = rows // 2
     weight_rows = up_ref.shape[0]
     tokens = x_ref.shape[0]
-    hidden = wup_ref.shape[1]
+    hidden = wup_s.shape[1]
     width = watt_s.shape[1] // 4
     block = 2 * rows
     blocks = tokens // block
     piece = 512
     place.greet()
+    shipped = []
+
+    def ship(source, target):
+        shipped.append(pltpu.make_async_copy(source, target, out_sem.at[len(shipped)]))
+        shipped[-1].start()
 
     def copy(t, kind, owner, part, own=False):
         target = targets[t].at[at_rows(owner * rows + part * half, half)]
@@ -325,66 +356,56 @@
 
     weights = Exchange(place, chunk, received, wsend, wreceive, wlocal)
 
-    def spread_out(t):
-        for distance in range(1, line):
-            along(t, distance)
-            beside(t, distance - 1)
-        beside(t, line - 1)
-
     own_copy(0).start()
     own_copy(1).start()
     along(0, 0)
     for owner in range(4 * line):
         columns = pl.ds(owner * width, width)
         packed[owner, :, :] = jnp.concatenate(
-            [qkv_ref[:, kind, columns] for kind in range(3)] + [out_ref[:, columns]], axis=1
-        )
-    spread_out(0)
+            [qkv_ref[kind, :, columns] for kind in range(3)] + [out_ref[:, columns]], axis=1
+        )
+    weights.keep((0, 1, 2))
+    for distance in range(1, line):
+        along(0, distance)
+        beside(0, distance - 1)
+    beside(0, line - 1)
     along(1, 0)
     weights.start((0,))
-    spread_out(1)
-    weights.start((1, 2))
+    for distance in range(1, line - 1):
+        along(1, distance)
+        beside(1, distance - 1)
+    weights.start((1, 2), lambda at, mask: not mask & 2)
     from_other(0)
     complete(0)
     weights.wait((0,))
-
-    def rows_in(source, at, slot):
-        return pltpu.make_async_copy(
-            source.at[at_rows(at * block, block)], buf.at[slot], buf_sem.at[slot]
-        )
-
-    def normed_out(at):
-        here = at_rows(at * block, block)
-        return pltpu.make_async_copy(normed_s.at[here], normed_ref.at[here], out_sem)
-
-    def step_rows(source, at):
-        slot = lax.rem(at, 2)
-        rows_in(source, at, slot).wait()
-
-        @pl.when(at + 1 < blocks)
-        def _():
-            rows_in(source, at + 1, 1 - slot).start()
-
-        return slot, at_rows(at * block, block)
+    ship(x_ref, x_out)
+    ship(watt_s, watt_out)
 
     quarter = tokens // inverse_ref.shape[0]
     quarters = block // quarter
-    rows_in(x_ref, 0, 0).start()
 
     def project(at, carry):
-        slot, here = step_rows(x_ref, at)
-        mean, inv_std = row_stats(buf, slot, features, piece)
+        here = at_rows(at * block, block)
+
+        def load(start):
+            return x_ref[here, pl.ds(start, piece)].astype(F32)
+
+        mean, inv_std = row_stats(load, block, features, piece)
         for start in range(0, features, piece):
             part = pl.ds(start, piece)
-            unit = (buf[slot, :, start : start + piece].astype(F32) - mean) * inv_std
+            unit = (load(start) - mean) * inv_std
             normed_s[here, part] = (unit * gain_ref[:, part] + shift_ref[:, part]).astype(BF)
         mixed = mm(normed_s[here, :], watt_s[...]) + batt_ref[...]
         mixed_s[pl.ds(at * quarters, quarters)] = mixed.reshape(quarters, quarter, 4 * width)
         return carry
 
-    lax.fori_loop(0, blocks, project, 0)
-    whole_normed = pltpu.make_async_copy(normed_s, normed_ref, out_sem)
-    whole_normed.start()
+    lax.fori_loop(0, blocks // 2, project, 0)
+    along(1, line - 1)
+    beside(1, line - 2)
+    lax.fori_loop(blocks // 2, blocks, project, 0)
+    ship(normed_s, normed_out)
+    beside(1, line - 1)
+    weights.start((1, 2), lambda at, mask: mask & 2)
 
     wide = 2 * block
     scale = 1.0 / math.sqrt(HEAD)
@@ -444,6 +465,8 @@
         return carry
 
     lax.fori_loop(0, blocks, forward, 0)
+    for source, target in ((qkvs_ref, qkvs_out), (lse_ref, lse_out), (attt_ref, attt_out)):
+        ship(source, target)
 
     def unplace(at, carry):
         attended = att_s[order_ref[at]][:, HEAD:]
@@ -453,18 +476,20 @@
         return carry
 
     lax.fori_loop(0, tokens // quarter, unplace, 0)
+    ship(att_ref, att_out)
     from_other(1)
     complete(1)
-    rows_in(g_ref, 0, 0).start()
+    ship(g_ref, g_out)
 
     def grad_in(at, carry):
-        slot, here = step_rows(g_ref, at)
-        grad = mm(buf[slot], watt_s[...]).astype(BF)
+        grad = mm(g_ref[at_rows(at * block, block), :], watt_s[...]).astype(BF)
         gatt_ref[pl.ds(at * quarters, quarters)] = grad.reshape(quarters, quarter, 4 * width)
         return carry
 
     lax.fori_loop(0, blocks, grad_in, 0)
+    ship(gatt_ref, gatt_out)
     weights.wait((1,))
+    ship(wup_s, wup_out)
 
     def feed(at, carry):
         here = at_rows(at * block, block)
@@ -474,8 +499,8 @@
         return carry
 
     lax.fori_loop(0, blocks, feed, 0)
-    watt_ref[...] = watt_s[...]
-    wup_ref[...] = wup_s[...]
+    ship(upward_ref, upward_out)
+    ship(act_ref, act_out)
     for t in range(2):
 
         def left(at, carry, t=t):
@@ -491,8 +516,9 @@
             return carry
 
         lax.fori_loop(0, line, left, 0)
-    whole_normed.wait()
     weights.wait((2,))
+    for result in shipped:
+        result.wait()
 
 
 def collect(
@@ -527,14 +553,22 @@
             shape((halves, total // halves, 4 * width), BF),
         ],
         in_specs=[smem, smem, hbm, hbm, vmem, vmem, hbm, hbm] + [vmem] * 5,
-        out_specs=[hbm, hbm, vmem, vmem, hbm, hbm] + [vmem] * 7,
+        out_specs=[hbm] * 13,
         scratch_shapes=[
-            pltpu.VMEM((count, weight_rows, 4 * width), BF),
+            pltpu.VMEM((total, features), BF),
+            pltpu.VMEM((total, features), BF),
             pltpu.VMEM((depth, 4 * width), BF),
             pltpu.VMEM((depth, hidden), BF),
             pltpu.VMEM((total, features), BF),
+            pltpu.VMEM((total, 4 * width), BF),
+            pltpu.VMEM((8, total), F32),
+            pltpu.VMEM((width, total), F32),
+            pltpu.VMEM((total, 4 * width), BF),
+            pltpu.VMEM((total, hidden), BF),
+            pltpu.VMEM((total, hidden), F32),
+            pltpu.VMEM((halves, total // halves, 4 * width), BF),
+            pltpu.VMEM((count, weight_rows, 4 * width), BF),
             pltpu.VMEM((halves, total // halves, 4 * width), F32),
-            pltpu.VMEM((2, 2 * rows, features), BF),
             pltpu.VMEM((total, width), BF),
             pltpu.VMEM((width, total), BF),
             pltpu.VMEM((total, 2 * rows), F32),
@@ -545,26 +579,27 @@
             dma((3, count)),
             dma((3, count)),
             dma((3,)),
-            dma((2,)),
-            dma,
+            dma((12,)),
         ],
         compiler_params=pltpu.CompilerParams(
-            collective_id=1, has_side_effects=True, vmem_limit_bytes=56 * 1024 * 1024
+            collective_id=1, has_side_effects=True, vmem_limit_bytes=60 * 1024 * 1024
         ),
     )(
-        order, inverse, tokens, cotangent, qkv_weight, out_weight, fc1_weight, fc2_weight, gain, shift,
-        bias_att, bias_up, angles,
+        order, inverse, tokens, cotangent, qkv_weight.transpose(1, 0, 2), out_weight, fc1_weight,
+        fc2_weight, gain, shift, bias_att, bias_up, angles,
     )
 
 
 def spread_kernel(
-    line, order_ref, inverse_ref, att_ref, act_ref, upward_ref, gatt_ref, qkvs_ref, lse_ref, attt_ref,
-    watt_ref, wup_ref, wdown_ref, angle_ref, normed_ref, g_ref, x_ref,
+    line, order_ref, inverse_ref, att_ref, act_ref, watt_ref, wdown_ref, lse_ref, angle_ref,
+    upward_in, gatt_in, qkvs_in, attt_in, wup_in, normed_ref, g_ref, x_ref,
     sum_ref, gsum_ref, ratt_ref, rup_ref, rdown_ref, rbias_ref, norms_ref, total_ref,
-    fresh, own, from_core, from_other, from_across, from_line, done, turned_s, dsend, cols, buf,
-    gain_s, shift_s, nsend, nfrom, nline, bias_s, gmix_s, gup_s, kt_s, dkv_s, gm_s,
-    cols_sem, buf_sem, csend, creceive, ysend, yreceive, xsend, xreceive, zsend, zreceive, fsend,
-    freceive, wsend, wreceive, wlocal, nsend_sem, nreceive, lsend, lreceive,
+    upward_ref, gatt_ref, qkvs_ref, attt_ref, wup_ref,
+    fresh, own, from_core, from_other, from_across, from_beyond, from_line, done, turned_s, dsend, cols,
+    buf, gain_s, shift_s, nsend, nfrom, nline, bias_s, gmix_s, gup_s, kt_s, dkv_s, gm_s,
+    in_sem, cols_sem, buf_sem, csend, creceive, credit, ysend, yreceive, xsend, xreceive, bsend,
+    breceive, zsend, zreceive, fsend, freceive, wsend, wreceive, wlocal, nsend_sem, nreceive, lsend,
+    lreceive,
 ):
     place = Place(line)
     a, b, c, y = place.a, place.b, place.c, place.y
@@ -578,7 +613,20 @@
     weight_rows = dsend.shape[1] // (2 * chips)
     pair = 2 * weight_rows
     piece = 512
+    ring = from_core.shape[0]
+    shortcut = 2 if line > 2 else -1
     place.greet()
+    late = [
+        pltpu.make_async_copy(source, target, in_sem.at[n])
+        for n, (source, target) in enumerate(
+            (
+                (upward_in, upward_ref), (gatt_in, gatt_ref), (qkvs_in, qkvs_ref), (attt_in, attt_ref),
+                (wup_in, wup_ref),
+            )
+        )
+    ]
+    for operand in late:
+        operand.start()
     mine, theirs = at_rows(y * half, half), at_rows((1 - y) * half, half)
     both, sibling = at_rows(c * rows, rows), at_rows((1 - c) * rows, rows)
 
@@ -598,8 +646,8 @@
 
     def to_core(t, turn):
         return remote(
-            fresh.at[lax.rem(turn, 2), sibling], from_core.at[t, order(turn)[1]], csend.at[t, turn],
-            creceive.at[t, order(turn)[1]], place.device[CORE],
+            fresh.at[lax.rem(turn, 2), sibling], from_core.at[lax.rem(turn, ring)], csend.at[t, turn],
+            creceive.at[lax.rem(turn, ring)], place.device[CORE],
         )
 
     def to_other(t, chip):
@@ -612,6 +660,12 @@
         return remote(
             own.at[t, at * 2 + 1 - b, mine], from_across.at[t, at], xsend.at[t, at], xreceive.at[t, at],
             place.device[ACROSS],
+        )
+
+    def to_beyond(t):
+        at = place.far_first(shortcut)
+        return remote(
+            own.at[t, at * 2 + 1 - b], from_beyond.at[t], bsend.at[t], breceive.at[t], place.device[ACROSS]
         )
 
     def to_up(t, at):
@@ -635,19 +689,29 @@
     def add(t, chip, part, other):
         own[t, chip, part, :] = (own[t, chip, part, :].astype(F32) + other.astype(F32)).astype(BF)
 
-    def columns_in(source, n, chip, slot):
-        return pltpu.make_async_copy(
-            source.at[:, at_rows(chip * pair, pair)], cols.at[n, slot], cols_sem.at[n, slot]
-        )
-
-    def rows_in(source, at, slot):
-        return pltpu.make_async_copy(
-            source.at[at_rows(at * block, block)], buf.at[slot], buf_sem.at[slot]
-        )
-
-    rows_in(g_ref, 0, 0).start()
-    for n, source in enumerate((normed_ref, g_ref)):
-        columns_in(source, n, 0, 0).start()
+    def columns_of(n, source):
+        return Stream(
+            lambda chip, slot: pltpu.make_async_copy(
+                source.at[:, at_rows(chip * pair, pair)], cols.at[n, slot], cols_sem.at[n, slot]
+            ),
+            cols.shape[1],
+            chips,
+        )
+
+    def rows_of(source, chip_of):
+        return Stream(
+            lambda at, slot: pltpu.make_async_copy(
+                source.at[at_rows(chip_of(at) * block, block)], buf.at[slot], buf_sem.at[slot]
+            ),
+            buf.shape[0],
+            blocks,
+        )
+
+    g_rows, x_rows = rows_of(g_ref, lambda at: at), rows_of(x_ref, lambda at: order(at)[1])
+    normed_columns, g_columns = columns_of(0, normed_ref), columns_of(1, g_ref)
+    g_rows.prime()
+    normed_columns.prime()
+    g_columns.prime()
 
     def product(t, turn):
         _, chip = order(turn)
@@ -657,34 +721,59 @@
         right = ((watt_ref, wdown_ref), (watt_ref, wup_ref))[t]
         first, second = left[0][here, :], left[1][here, :]
         if t == 1:
-            slot = lax.rem(turn, 2)
-            rows_in(x_ref, chip, slot).wait()
-
-            @pl.when(turn + 1 < chips)
-            def _():
-                rows_in(x_ref, order(turn + 1)[1], 1 - slot).start()
-
-            mean, inv_std = row_stats(buf, slot, features, piece)
+            slot = x_rows.step(turn)
+
+            def load(start):
+                return buf[slot, :, pl.ds(start, piece)].astype(F32)
+
+            mean, inv_std = row_stats(load, block, features, piece)
         for start in range(0, features, piece):
             part = pl.ds(start, piece)
             value = mm(first, right[0][part, :], NT) + mm(second, right[1][part, :], NT)
             fresh[fresh_at, :, part] = value.astype(BF)
             if t == 1:
-                unit = (buf[slot, :, start : start + piece].astype(F32) - mean) * inv_std
+                unit = (load(start) - mean) * inv_std
                 shift_s[:, part] += jnp.sum(value.reshape(block // 8, 8, piece), axis=0)
                 gain_s[:, part] += jnp.sum((unit * value).reshape(block // 8, 8, piece), axis=0)
+        if t == 1:
+            pl.semaphore_wait(credit, 1)
+        else:
+            pl.when(turn >= ring)(lambda: pl.semaphore_wait(credit, 1))
         to_core(t, turn).start()
 
     def stage_core(t, turn):
         _, chip = order(turn)
         to_core(t, turn).wait_recv()
         own[t, chip, :, :] = (
-            fresh[lax.rem(turn, 2), both, :].astype(F32) + from_core[t, chip].astype(F32)
+            fresh[lax.rem(turn, 2), both, :].astype(F32)
+            + from_core[lax.rem(turn, ring)].astype(F32)
         ).astype(BF)
+
+        def give():
+            pl.semaphore_signal(
+                credit, inc=1, device_id=place.device[CORE], device_id_type=MESH
+            )
+
+        if t == 0:
+            give()
+        else:
+            pl.when(turn < chips - ring)(give)
+        if shortcut < 0:
+            to_other(t, chip).start()
+        else:
+            pl.when(turn == 2 * shortcut)(lambda: to_beyond(t).start())
+            pl.when(turn // 2 != shortcut)(lambda: to_other(t, chip).start())
+        to_core(t, turn).wait_send()
+
+    def stage_beyond(t):
+        chip = place.far_first(shortcut) * 2 + b
+        to_beyond(t).wait_recv()
+        add(t, chip, pl.ds(0, rows), from_beyond[t])
         to_other(t, chip).start()
-        to_core(t, turn).wait_send()
 
     def stage_other(t, nth):
+        if nth == shortcut:
+            return
         at = place.far_first(nth)
         chip = at * 2 + 1 - b
         to_other(t, chip).wait_recv()
@@ -695,8 +784,11 @@
         at = place.far_first(nth)
         chip = at * 2 + b
         to_other(t, chip).wait_recv()
-        to_across(t, at).wait_recv()
-        add(t, chip, mine, from_other[t, chip].astype(F32) + from_across[t, at].astype(F32))
+        if nth == shortcut:
+            add(t, chip, mine, from_other[t, chip])
+        else:
+            to_across(t, at).wait_recv()
+            add(t, chip, mine, from_other[t, chip].astype(F32) + from_across[t, at].astype(F32))
 
         def down():
             @pl.when(a < line - 1)
@@ -733,14 +825,6 @@
         done[t, mine, :] = own[t, chip, mine, :]
         final(t, mine).start()
 
-    def stages(t):
-        steps = [functools.partial(stage_other, t, 0)]
-        for nth in range(1, line):
-            steps.append(functools.partial(stage_other, t, nth))
-            steps.append(functools.partial(stage_line, t, nth - 1))
-        steps.append(functools.partial(stage_line, t, line - 1))
-        return steps
-
     def norm_copy(step):
         kind = (CORE, OTHER, ACROSS)[step]
         return remote(
@@ -762,16 +846,11 @@
 
     lax.fori_loop(1, chips, first_sum, 0)
     stage_core(0, chips - 1)
-    pending = stages(0)
+
+    late[0].wait()
 
     def feed_back(at, carry):
-        slot = lax.rem(at, 2)
-        rows_in(g_ref, at, slot).wait()
-
-        @pl.when(at + 1 < blocks)
-        def _():
-            rows_in(g_ref, at + 1, 1 - slot).start()
-
+        slot = g_rows.step(at)
         here = at_rows(at * block, block)
         upward = upward_ref[here, :]
         tanh = gelu_parts(upward)
@@ -782,9 +861,11 @@
         return carry
 
     lax.fori_loop(0, blocks // 2, feed_back, 0)
-    pending.pop(0)()
+    stage_other(0, 0)
     lax.fori_loop(blocks // 2, blocks, feed_back, 0)
-    rows_in(x_ref, order(0)[1], 0).start()
+    if shortcut >= 0:
+        stage_beyond(0)
+    x_rows.prime()
 
     def turn_over(pieces):
         def one(at, carry):
@@ -799,14 +880,8 @@
     ones = jnp.ones((8, tokens), BF)
 
     def gradients(chip, carry):
-        slot = lax.rem(chip, 2)
-        for n, source in enumerate((normed_ref, g_ref)):
-            columns_in(source, n, chip, slot).wait()
-
-            @pl.when(chip + 1 < chips)
-            def _(n=n, source=source):
-                columns_in(source, n, chip + 1, 1 - slot).start()
-
+        slot = normed_columns.step(chip)
+        g_columns.step(chip)
         here = at_rows(chip * pair, pair)
         by_normed, by_grad = cols[0, slot], cols[1, slot]
         dsend[0, here, :] = mm(turned_s[2], by_grad).T.astype(BF)
@@ -816,11 +891,14 @@
         return carry
 
     lax.fori_loop(0, chips // 2, gradients, 0)
-    pending.pop(0)()
+    stage_other(0, 1)
     lax.fori_loop(chips // 2, chips, gradients, 0)
+    weights.keep((1, 2))
     weights.start((1, 2))
-    columns_in(normed_ref, 0, 0, 0).start()
-    pending.pop(0)()
+    normed_columns.prime()
+    for operand in late[1:]:
+        operand.wait()
+    others_left = list(range(2, line))
 
     quarter = tokens // inverse_ref.shape[0]
     quarters = block // quarter
@@ -876,11 +954,11 @@
         )
         return carry
 
-    done_blocks = 0
-    for upto in (blocks // 2, blocks * 3 // 4, blocks * 7 // 8, blocks):
-        lax.fori_loop(done_blocks, upto, backward, 0)
-        done_blocks = upto
-        pending.pop(0)()
+    lax.fori_loop(0, blocks // 2, backward, 0)
+    for nth in others_left[:-1]:
+        stage_other(0, nth)
+    lax.fori_loop(blocks // 2, blocks, backward, 0)
+    stage_other(0, line - 1)
 
     def finish_keys(at, carry):
         here = at_rows(at * block, block)
@@ -926,13 +1004,7 @@
     shift_s[...] = jnp.zeros_like(shift_s)
 
     def gradients_att(chip):
-        slot = lax.rem(chip, 2)
-        columns_in(normed_ref, 0, chip, slot).wait()
-
-        @pl.when(chip + 1 < chips)
-        def _():
-            columns_in(normed_ref, 0, chip + 1, 1 - slot).start()
-
+        slot = normed_columns.step(chip)
         here = at_rows(chip * pair, pair)
         more = mm(turned_s[0], cols[0, slot]).T
         dsend[0, here, :] = (dsend[0, here, :].astype(F32) + more).astype(BF)
@@ -948,34 +1020,37 @@
     lax.fori_loop(1, chips, second_sum, 0)
     stage_core(1, chips - 1)
     gradients_att(chips - 1)
-    weights.start((0, 3))
-    for step in pending:
-        step()
     for n, source in enumerate((gain_s, shift_s)):
         total = jnp.sum(source[...], axis=0, keepdims=True)
         span = features // 4
         for at in range(4):
             nsend[0, pl.ds(n * 4 + at, 1), :] = total[:, at * span : (at + 1) * span]
     norm_copy(0).start()
-    pending = stages(1)
-    pending.pop(0)()
+    if shortcut >= 0:
+        stage_beyond(1)
+    weights.keep((0, 3))
+    share = -(-2 * chips // line)
+    for nth in range(line):
+        if nth < line - 1:
+            stage_other(1, nth)
+        stage_line(0, nth)
+        weights.start((0, 3), lambda at, mask, nth=nth: at // share == nth)
     norm_copy(0).wait_recv()
     nsend[1] = nsend[0] + nfrom[0]
     norm_copy(1).start()
-    pending.pop(0)()
-    pending.pop(0)()
+    stage_line(1, 0)
     norm_copy(1).wait_recv()
     nsend[2] = nsend[1] + nfrom[1]
     norm_copy(2).start()
-    pending.pop(0)()
-    pending.pop(0)()
+    stage_line(1, 1)
     norm_copy(2).wait_recv()
     nsend[3] = nsend[2] + nfrom[2]
     nline[a] = nsend[3]
     for other in range(line):
         pl.when(a != other)(lambda other=other: norm_line(other, False).start())
-    for step in pending:
-        step()
+    stage_other(1, line - 1)
+    for nth in range(2, line):
+        stage_line(1, nth)
     for other in range(line):
         pl.when(a != other)(lambda other=other: norm_line(other, True).wait_recv())
     total = nline[0]
@@ -993,13 +1068,22 @@
         sums[t][...] = done[t]
 
         def left(at, carry, t=t):
-            to_other(t, at * 2).wait_send()
-            to_other(t, at * 2 + 1).wait_send()
-            to_across(t, at).wait_send()
+            to_other(t, at * 2 + b).wait_send()
             pl.when(at != a)(lambda: to_up(t, at).wait_send())
+
+            def also():
+                to_other(t, at * 2 + 1 - b).wait_send()
+                to_across(t, at).wait_send()
+
+            if shortcut < 0:
+                also()
+            else:
+                pl.when(at != place.far_first(shortcut))(also)
             return carry
 
         lax.fori_loop(0, line, left, 0)
+        if shortcut >= 0:
+            to_beyond(t).wait_send()
     weights.wait((0, 1, 2, 3))
 
 
@@ -1031,20 +1115,26 @@
             jax.ShapeDtypeStruct((8, features // 4), F32),
             jax.ShapeDtypeStruct((8, features), F32),
         ],
-        in_specs=[smem, smem] + [vmem] * 11 + [hbm] * 3,
+        in_specs=[smem, smem] + [vmem] * 6 + [hbm] * 8,
         out_specs=[vmem, vmem, hbm, hbm, hbm, hbm, vmem, vmem],
         scratch_shapes=[
+            pltpu.VMEM(upward.shape, F32),
+            pltpu.VMEM(grad_att.shape, BF),
+            pltpu.VMEM(qkvs.shape, BF),
+            pltpu.VMEM(attended_t.shape, F32),
+            pltpu.VMEM(w_up.shape, BF),
             pltpu.VMEM((2, 2 * rows, features), BF),
             pltpu.VMEM((2, chips, rows, features), BF),
-            pltpu.VMEM((2, chips, rows, features), BF),
+            pltpu.VMEM((4, rows, features), BF),
             pltpu.VMEM((2, chips, half, features), BF),
             pltpu.VMEM((2, line, half, features), BF),
+            pltpu.VMEM((2, rows, features), BF),
             pltpu.VMEM((2, line + 1, half, features), BF),
             pltpu.VMEM((2, rows, features), BF),
             pltpu.VMEM((4, wide, tokens), BF),
             pltpu.VMEM((3, count * weight_rows, wide), BF),
-            pltpu.VMEM((2, 2, tokens, 2 * weight_rows), BF),
-            pltpu.VMEM((2, 2 * rows, features), BF),
+            pltpu.VMEM((2, 3, tokens, 2 * weight_rows), BF),
+            pltpu.VMEM((3, 2 * rows, features), BF),
             pltpu.VMEM((8, features), F32),
             pltpu.VMEM((8, features), F32),
             pltpu.VMEM((4, 8, features // 4), F32),
@@ -1056,14 +1146,18 @@
             pltpu.VMEM((HEAD, tokens), BF),
             pltpu.VMEM((tokens, 2 * HEAD), F32),
             pltpu.VMEM((order.shape[0], tokens // order.shape[0], 3 * HEAD), BF),
-            dma((2, 2)),
-            dma((2,)),
+            dma((5,)),
+            dma((2, 3)),
+            dma((3,)),
             dma((2, chips)),
-            dma((2, chips)),
+            dma((4,)),
+            pltpu.SemaphoreType.REGULAR,
             dma((2, chips)),
             dma((2, chips)),
             dma((2, line)),
             dma((2, line)),
+            dma((2,)),
+            dma((2,)),
             dma((2, line)),
             dma((2, line + 1)),
             dma((2,)),
@@ -1080,8 +1174,8 @@
             collective_id=2, has_side_effects=True, vmem_limit_bytes=63 * 1024 * 1024
         ),
     )(
-        order, inverse, attended, activated, upward, grad_att, qkvs, lse, attended_t, w_att, w_up,
-        w_down, angles, normed, g_all, x_all,
+        order, inverse, attended, activated, w_att, w_down, lse, angles, upward, grad_att, qkvs,
+        attended_t, w_up, normed, g_all, x_all,
     )
 
 
@@ -1104,17 +1198,28 @@
     )
     count, _, packed = datt_ref.shape
     width, hidden = packed // 4, dup_ref.shape[2]
+    pieces = [datt_ref[owner].astype(F32) for owner in range(count)]
+
+    def together(kind):
+        return jnp.concatenate(
+            [piece[:, kind * width : (kind + 1) * width] for piece in pieces], axis=1
+        )
+
+    for kind in range(3):
+        qkv_ref[kind, :, :] = together(kind)
+        at = kind * width
+        qkvb_ref[kind : kind + 1, :] = jnp.concatenate(
+            [
+                sums_ref[owner, at // 128 : at // 128 + 1, at % 128 : at % 128 + width]
+                for owner in range(count)
+            ],
+            axis=1,
+        )
+    wout_ref[...] = together(3)
     for owner in range(count):
-        columns = pl.ds(owner * width, width)
-        piece = datt_ref[owner].astype(F32)
-        for kind in range(3):
-            qkv_ref[:, kind, columns] = piece[:, kind * width : (kind + 1) * width]
-        wout_ref[:, columns] = piece[:, 3 * width :]
-        up_ref[:, pl.ds(owner * hidden, hidden)] = dup_ref[owner].astype(F32)
-        down_ref[:, pl.ds(owner * hidden, hidden)] = ddown_ref[owner].astype(F32)
-        for kind in range(3):
-            at = kind * width
-            qkvb_ref[pl.ds(kind, 1), columns] = sums_ref[owner, at // 128 : at // 128 + 1, at % 128 : at % 128 + width]
+        columns = pl.ds(owner * hidden, hidden)
+        up_ref[:, columns] = dup_ref[owner].astype(F32)
+        down_ref[:, columns] = ddown_ref[owner].astype(F32)
         for at in range(hidden // 128):
             upb_ref[:, pl.ds(owner * hidden + at * 128, 128)] = sums_ref[owner, 2 + at : 3 + at, :]
     wide = norms_ref.shape[1]
@@ -1126,27 +1231,58 @@
 
 def finish(tokens, cotangent, gain, bias, branches, own_normed, d_att, d_up, d_down, sums, norms, total):
     count, weight_rows, packed = d_att.shape
+    rows, features = tokens.shape
     width, hidden = packed // 4, d_up.shape[2]
-    vmem = pl.BlockSpec(memory_space=pltpu.VMEM)
-    rows = jax.ShapeDtypeStruct(tokens.shape, F32)
+    owners = max(128 // width, count * 16 // rows)
+    steps = count // owners
+    by_rows = pl.BlockSpec((rows // steps, features), lambda at: (at, 0))
+    line = pl.BlockSpec((1, features), lambda at: (0, 0))
+
+    def whole(array):
+        return pl.BlockSpec(array.shape, lambda at: (0,) * array.ndim)
+
+    def by_owner(array):
+        return pl.BlockSpec((owners, *array.shape[1:]), lambda at: (at, 0, 0))
+
+    def by_columns(*lead):
+        return lambda columns: pl.BlockSpec(
+            (*lead, owners * columns), lambda at: (*(0,) * len(lead), at)
+        )
+
+    shape = jax.ShapeDtypeStruct
     return pl.pallas_call(
         finish_kernel,
+        grid=(steps,),
         out_shape=[
-            rows,
-            rows,
-            jax.ShapeDtypeStruct((weight_rows, 3, count * width), F32),
-            jax.ShapeDtypeStruct((weight_rows, count * width), F32),
-            jax.ShapeDtypeStruct((weight_rows, count * hidden), F32),
-            jax.ShapeDtypeStruct((weight_rows, count * hidden), F32),
-            jax.ShapeDtypeStruct((3, count * width), F32),
-            jax.ShapeDtypeStruct((1, count * hidden), F32),
-            jax.ShapeDtypeStruct((1, tokens.shape[1]), F32),
-            jax.ShapeDtypeStruct((1, tokens.shape[1]), F32),
-            jax.ShapeDtypeStruct((1, tokens.shape[1]), F32),
+            shape(tokens.shape, F32),
+            shape(tokens.shape, F32),
+            shape((3, weight_rows, count * width), F32),
+            shape((weight_rows, count * width), F32),
+            shape((weight_rows, count * hidden), F32),
+            shape((weight_rows, count * hidden), F32),
+            shape((3, count * width), F32),
+            shape((1, count * hidden), F32),
+            shape((1, features), F32),
+            shape((1, features), F32),
+            shape((1, features), F32),
         ],
-        in_specs=[vmem] * 12,
-        out_specs=[vmem] * 11,
-        compiler_params=pltpu.CompilerParams(vmem_limit_bytes=50 * 1024 * 1024),
+        in_specs=[by_rows, by_rows, line, line, by_rows, by_rows]
+        + [by_owner(array) for array in (d_att, d_up, d_down, sums)]
+        + [whole(norms), whole(total)],
+        out_specs=[
+            by_rows,
+            by_rows,
+            by_columns(3, weight_rows)(width),
+            by_columns(weight_rows)(width),
+            by_columns(weight_rows)(hidden),
+            by_columns(weight_rows)(hidden),
+            by_columns(3)(width),
+            by_columns(1)(hidden),
+            line,
+            line,
+            line,
+        ],
+        compiler_params=pltpu.CompilerParams(vmem_limit_bytes=63 * 1024 * 1024),
     )(
         tokens, cotangent, gain[None], bias[None], branches, own_normed, d_att, d_up, d_down, sums,
         norms, total,
@@ -1200,8 +1336,8 @@
         shift_sum, g_sum,
     ) = finish(tokens, cotangent, ln_gain, out_bias, *parts)
     return (
-        output, input_grad, gain_sum[0], shift_sum[0], qkv_grad, qkv_sums, out_grad, fc1_grad,
-        fc1_sums[0], fc2_grad, g_sum[0],
+        output, input_grad, gain_sum[0], shift_sum[0], qkv_grad.transpose(1, 0, 2), qkv_sums, out_grad,
+        fc1_grad, fc1_sums[0], fc2_grad, g_sum[0],
     )
 
 

time: 364 us -> 309 us (0.85)
  Pallas kernels: 345 us -> 303 us
  local copies, waits for them, and re-layouts: 15.4 us -> 3.37 us
    pallas_call x1, Pallas kernels: 157 us -> 130 us  [collect(): pl.pallas_call(functools.partial(collect_kernel, line), out_shape=[shape(...]
    pallas_call x1, Pallas kernels: 179 us -> 163 us  [spread(): pl.pallas_call(functools.partial(spread_kernel, line), out_shape=[own, ow...]
    unnamed x26 -> x2, local copies, waits for them, and re-layouts: 12.1 us -> 0.01 us
where the time goes in v1:
time: 309 us
  Pallas kernels  303 us (98%)
  local copies, waits for them, and re-layouts  3.37 us (1%)
    pallas_call x1, Pallas kernels, spread(): pl.pallas_call(functools.partial(spread_kernel, line), out_shape=[own, ow...  163 us
    pallas_call x1, Pallas kernels, collect(): pl.pallas_call(functools.partial(collect_kernel, line), out_shape=[shape(...  130 us
    pallas_call x1, Pallas kernels, finish(): pl.pallas_call(finish_kernel, grid=(steps,), out_shape=[shape(tokens.shap...  9.39 us

profile of v1, /device:TPU:0, one launch (start us, length us, event | category | flops | bytes accessed | tf_op | source)
XLA Modules:
  0.0 308.9 jit_solution(11985223650007733701)
XLA Ops:
  0.6 0.0 copy-start
  0.7 1.3 select_reduce_fusion.inverse_ref
  2.0 1.3 dynamic_slice.7
  3.3 0.0 copy-done
  3.3 0.1 constant_dynamic-slice_fusion
  3.4 0.1 reshape.37
  3.5 0.6 concatenate.6
  4.0 0.5 multiply_cosine_fusion
  4.6 1.3 copy.25.angle_ref
  5.9 130.1 %shard_map.203 = (bf16[2048,2048]{1,0:T(8,128)(2,1)}, bf16[2048,2048]{1,0:T(8,128)(2,1)}, bf16[2048,256]{1,0:T(8,128)(2,1)}, bf16[2048,256]{1,0:T(8,128)(2,1)}, ...) custom-call(s32[32]{0:T(128)} %order_ref.3, ...), custom_call_target="tpu_custom_call" | custom-call | tf_op jit(solution)/shard_map/pallas_call | solution.py:538
  136.0 163.4 %shard_map.204 = (bf16[128,2048]{1,0:T(8,128)(2,1)}, bf16[128,2048]{1,0:T(8,128)(2,1)}, bf16[16,128,256]{2,1,0:T(8,128)(2,1)}, bf16[16,128,256]{2,1,0:T(8,128)(2...) custom-call(s32[32]{0:T(128)} %order_ref.3, ...), custom_call_target="tpu_custom_call" | custom-call | tf_op jit(solution)/shard_map/pallas_call | solution.py:1109
  299.4 9.4 %shard_map.205 = (f32[128,2048]{1,0:T(8,128)}, f32[128,2048]{1,0:T(8,128)}, f32[3,128,1024]{2,1,0:T(8,128)}, f32[128,1024]{1,0:T(8,128)}, f32[128,4096]{1,0:T(8,...) custom-call(bf16[128,2048]{1,0:T(8,128)(2,1)} %tok_ref.3, ...), custom_call_target="tpu_custom_call" | custom-call | tf_op jit(solution)/shard_map/pallas_call | solution.py:1253
  (3 shorter events, 0.0 us)
Async XLA Ops:
  0.6 2.7 copy-start

commit v2 on v1

--- a/solution.py
+++ b/solution.py
@@ -3,6 +3,7 @@
 
 import jax
 import jax.numpy as jnp
+import numpy as np
 from jax import lax
 from jax.experimental import pallas as pl
 from jax.experimental.pallas import tpu as pltpu
@@ -186,11 +187,10 @@
         for n in pieces:
             self.kept(n).start()
 
-    def start(self, pieces, wanted=lambda at, mask: True):
-        for at, partner in enumerate(self.partners):
+    def start(self, pieces):
+        for partner in self.partners:
             for n in pieces:
-                if wanted(at, partner[0]):
-                    self.copy(partner, n, False).start()
+                self.copy(partner, n, False).start()
 
     def wait(self, pieces):
         for partner in self.partners:
@@ -243,10 +243,10 @@
 
 
 def collect_kernel(
-    line, order_ref, inverse_ref, tok_ref, cot_ref, qkv_ref, out_ref, up_ref, down_ref, gain_ref,
+    line, order_ref, tok_ref, cot_ref, qkv_ref, out_ref, up_ref, down_ref, gain_ref,
     shift_ref, batt_ref, bup_ref, angle_ref,
     x_out, g_out, watt_out, wup_out, wdown_ref, normed_out, qkvs_out, lse_out, attt_out, att_out,
-    act_out, upward_out, gatt_out,
+    act_out, upward_out, gatt_out, inverse_ref,
     x_ref, g_ref, watt_s, wup_s, normed_s, qkvs_ref, lse_ref, attt_ref, att_ref, act_ref, upward_ref,
     gatt_ref, packed, mixed_s, k_s, vt_s, st, att_s,
     send, receive, own_sem, wsend, wreceive, wlocal, out_sem,
@@ -365,16 +365,25 @@
             [qkv_ref[kind, :, columns] for kind in range(3)] + [out_ref[:, columns]], axis=1
         )
     weights.keep((0, 1, 2))
+    ordered = [order_ref[at] for at in range(order_ref.shape[0])]
+
+    def invert(wanted, carry):
+        found = jnp.int32(0)
+        for at, held in enumerate(ordered):
+            found = jnp.where(held == wanted, at, found)
+        inverse_ref[wanted] = found
+        return carry
+
     for distance in range(1, line):
         along(0, distance)
         beside(0, distance - 1)
     beside(0, line - 1)
     along(1, 0)
     weights.start((0,))
+    lax.fori_loop(0, len(ordered), invert, 0)
     for distance in range(1, line - 1):
         along(1, distance)
         beside(1, distance - 1)
-    weights.start((1, 2), lambda at, mask: not mask & 2)
     from_other(0)
     complete(0)
     weights.wait((0,))
@@ -402,10 +411,11 @@
     lax.fori_loop(0, blocks // 2, project, 0)
     along(1, line - 1)
     beside(1, line - 2)
+    weights.start((1,))
     lax.fori_loop(blocks // 2, blocks, project, 0)
     ship(normed_s, normed_out)
     beside(1, line - 1)
-    weights.start((1, 2), lambda at, mask: mask & 2)
+    weights.start((2,))
 
     wide = 2 * block
     scale = 1.0 / math.sqrt(HEAD)
@@ -522,8 +532,8 @@
 
 
 def collect(
-    order, inverse, tokens, cotangent, qkv_weight, out_weight, fc1_weight, fc2_weight, gain, shift,
-    bias_att, bias_up, angles,
+    order, tokens, cotangent, qkv_weight, out_weight, fc1_weight, fc2_weight, gain, shift, bias_att,
+    bias_up, angles,
 ):
     rows, features = tokens.shape
     weight_rows = fc1_weight.shape[0]
@@ -551,9 +561,10 @@
             shape((total, hidden), BF),
             shape((total, hidden), F32),
             shape((halves, total // halves, 4 * width), BF),
+            shape((halves,), jnp.int32),
         ],
-        in_specs=[smem, smem, hbm, hbm, vmem, vmem, hbm, hbm] + [vmem] * 5,
-        out_specs=[hbm] * 13,
+        in_specs=[smem, hbm, hbm, vmem, vmem, hbm, hbm] + [vmem] * 5,
+        out_specs=[hbm] * 13 + [smem],
         scratch_shapes=[
             pltpu.VMEM((total, features), BF),
             pltpu.VMEM((total, features), BF),
@@ -585,7 +596,7 @@
             collective_id=1, has_side_effects=True, vmem_limit_bytes=60 * 1024 * 1024
         ),
     )(
-        order, inverse, tokens, cotangent, qkv_weight.transpose(1, 0, 2), out_weight, fc1_weight,
+        order, tokens, cotangent, qkv_weight.transpose(1, 0, 2), out_weight, fc1_weight,
         fc2_weight, gain, shift, bias_att, bias_up, angles,
     )
 
@@ -614,7 +625,7 @@
     pair = 2 * weight_rows
     piece = 512
     ring = from_core.shape[0]
-    shortcut = 2 if line > 2 else -1
+    shortcuts = tuple(range(line - from_beyond.shape[1], line))
     place.greet()
     late = [
         pltpu.make_async_copy(source, target, in_sem.at[n])
@@ -662,10 +673,11 @@
             place.device[ACROSS],
         )
 
-    def to_beyond(t):
-        at = place.far_first(shortcut)
+    def to_beyond(t, nth):
+        at, slot = place.far_first(nth), nth - shortcuts[0]
         return remote(
-            own.at[t, at * 2 + 1 - b], from_beyond.at[t], bsend.at[t], breceive.at[t], place.device[ACROSS]
+            own.at[t, at * 2 + 1 - b], from_beyond.at[t, slot], bsend.at[t, slot],
+            breceive.at[t, slot], place.device[ACROSS],
         )
 
     def to_up(t, at):
@@ -758,21 +770,20 @@
             give()
         else:
             pl.when(turn < chips - ring)(give)
-        if shortcut < 0:
+        pl.when(turn < 2 * shortcuts[0])(lambda: to_other(t, chip).start())
+        for nth in shortcuts:
+            pl.when(turn == 2 * nth)(lambda nth=nth: to_beyond(t, nth).start())
+        to_core(t, turn).wait_send()
+
+    def stage_beyond(t):
+        for nth in shortcuts:
+            chip = place.far_first(nth) * 2 + b
+            to_beyond(t, nth).wait_recv()
+            add(t, chip, pl.ds(0, rows), from_beyond[t, nth - shortcuts[0]])
             to_other(t, chip).start()
-        else:
-            pl.when(turn == 2 * shortcut)(lambda: to_beyond(t).start())
-            pl.when(turn // 2 != shortcut)(lambda: to_other(t, chip).start())
-        to_core(t, turn).wait_send()
-
-    def stage_beyond(t):
-        chip = place.far_first(shortcut) * 2 + b
-        to_beyond(t).wait_recv()
-        add(t, chip, pl.ds(0, rows), from_beyond[t])
-        to_other(t, chip).start()
 
     def stage_other(t, nth):
-        if nth == shortcut:
+        if nth in shortcuts:
             return
         at = place.far_first(nth)
         chip = at * 2 + 1 - b
@@ -784,7 +795,7 @@
         at = place.far_first(nth)
         chip = at * 2 + b
         to_other(t, chip).wait_recv()
-        if nth == shortcut:
+        if nth in shortcuts:
             add(t, chip, mine, from_other[t, chip])
         else:
             to_across(t, at).wait_recv()
@@ -846,6 +857,31 @@
 
     lax.fori_loop(1, chips, first_sum, 0)
     stage_core(0, chips - 1)
+
+    def turn_over(pieces):
+        def one(at, carry):
+            here = at_rows(at * 256, 256)
+            for n, source in pieces:
+                turned_s[n, :, here] = source[here, :].T
+            return carry
+
+        lax.fori_loop(0, tokens // 256, one, 0)
+
+    turn_over(((2, att_ref), (3, act_ref)))
+    ones = jnp.ones((8, tokens), BF)
+
+    def gradients_down(chip, carry):
+        slot = g_columns.step(chip)
+        here = at_rows(chip * pair, pair)
+        by_grad = cols[1, slot]
+        dsend[2, here, :] = mm(turned_s[3], by_grad).T.astype(BF)
+        dsend[0, here, :] = mm(turned_s[2], by_grad).T.astype(BF)
+        total_ref[:, here] = mm(ones, by_grad)
+        return carry
+
+    lax.fori_loop(0, chips, gradients_down, 0)
+    weights.keep((2,))
+    weights.start((2,))
 
     late[0].wait()
 
@@ -860,45 +896,24 @@
         gup_s[here, :] = (mm(buf[slot], wdown_ref[...]) * slope).astype(BF)
         return carry
 
-    lax.fori_loop(0, blocks // 2, feed_back, 0)
+    lax.fori_loop(0, blocks, feed_back, 0)
     stage_other(0, 0)
-    lax.fori_loop(blocks // 2, blocks, feed_back, 0)
-    if shortcut >= 0:
-        stage_beyond(0)
     x_rows.prime()
 
-    def turn_over(pieces):
-        def one(at, carry):
-            here = at_rows(at * 256, 256)
-            for n, source in pieces:
-                turned_s[n, :, here] = source[here, :].T
-            return carry
-
-        lax.fori_loop(0, tokens // 256, one, 0)
-
-    turn_over(((1, gup_s), (2, att_ref), (3, act_ref)))
-    ones = jnp.ones((8, tokens), BF)
-
-    def gradients(chip, carry):
+    turn_over(((1, gup_s),))
+
+    def gradients_up(chip, carry):
         slot = normed_columns.step(chip)
-        g_columns.step(chip)
-        here = at_rows(chip * pair, pair)
-        by_normed, by_grad = cols[0, slot], cols[1, slot]
-        dsend[0, here, :] = mm(turned_s[2], by_grad).T.astype(BF)
-        dsend[1, here, :] = mm(turned_s[1], by_normed).T.astype(BF)
-        dsend[2, here, :] = mm(turned_s[3], by_grad).T.astype(BF)
-        total_ref[:, here] = mm(ones, by_grad)
-        return carry
-
-    lax.fori_loop(0, chips // 2, gradients, 0)
+        dsend[1, at_rows(chip * pair, pair), :] = mm(turned_s[1], cols[0, slot]).T.astype(BF)
+        return carry
+
+    lax.fori_loop(0, chips, gradients_up, 0)
+    weights.keep((1,))
+    weights.start((1,))
     stage_other(0, 1)
-    lax.fori_loop(chips // 2, chips, gradients, 0)
-    weights.keep((1, 2))
-    weights.start((1, 2))
     normed_columns.prime()
     for operand in late[1:]:
         operand.wait()
-    others_left = list(range(2, line))
 
     quarter = tokens // inverse_ref.shape[0]
     quarters = block // quarter
@@ -955,10 +970,12 @@
         return carry
 
     lax.fori_loop(0, blocks // 2, backward, 0)
-    for nth in others_left[:-1]:
+    stage_beyond(0)
+    for nth in range(2, line - 1):
         stage_other(0, nth)
     lax.fori_loop(blocks // 2, blocks, backward, 0)
-    stage_other(0, line - 1)
+    if line > 2:
+        stage_other(0, line - 1)
 
     def finish_keys(at, carry):
         here = at_rows(at * block, block)
@@ -1014,27 +1031,30 @@
     def second_sum(turn, carry):
         product(1, turn)
         stage_core(1, turn - 1)
-        gradients_att(turn - 1)
-        return carry
-
-    lax.fori_loop(1, chips, second_sum, 0)
+        return carry
+
+    def second_sum_too(turn, carry):
+        second_sum(turn, carry)
+        gradients_att(2 * turn - 2)
+        gradients_att(2 * turn - 1)
+        return carry
+
+    lax.fori_loop(1, chips // 2 + 1, second_sum_too, 0)
+    weights.keep((0, 3))
+    weights.start((0, 3))
+    lax.fori_loop(chips // 2 + 1, chips, second_sum, 0)
     stage_core(1, chips - 1)
-    gradients_att(chips - 1)
     for n, source in enumerate((gain_s, shift_s)):
         total = jnp.sum(source[...], axis=0, keepdims=True)
         span = features // 4
         for at in range(4):
             nsend[0, pl.ds(n * 4 + at, 1), :] = total[:, at * span : (at + 1) * span]
     norm_copy(0).start()
-    if shortcut >= 0:
-        stage_beyond(1)
-    weights.keep((0, 3))
-    share = -(-2 * chips // line)
+    stage_beyond(1)
     for nth in range(line):
         if nth < line - 1:
             stage_other(1, nth)
         stage_line(0, nth)
-        weights.start((0, 3), lambda at, mask, nth=nth: at // share == nth)
     norm_copy(0).wait_recv()
     nsend[1] = nsend[0] + nfrom[0]
     norm_copy(1).start()
@@ -1075,15 +1095,15 @@
                 to_other(t, at * 2 + 1 - b).wait_send()
                 to_across(t, at).wait_send()
 
-            if shortcut < 0:
-                also()
-            else:
-                pl.when(at != place.far_first(shortcut))(also)
+            shorter = at == place.far_first(shortcuts[0])
+            for nth in shortcuts[1:]:
+                shorter = shorter | (at == place.far_first(nth))
+            pl.when(jnp.logical_not(shorter))(also)
             return carry
 
         lax.fori_loop(0, line, left, 0)
-        if shortcut >= 0:
-            to_beyond(t).wait_send()
+        for nth in shortcuts:
+            to_beyond(t, nth).wait_send()
     weights.wait((0, 1, 2, 3))
 
 
@@ -1128,7 +1148,7 @@
             pltpu.VMEM((4, rows, features), BF),
             pltpu.VMEM((2, chips, half, features), BF),
             pltpu.VMEM((2, line, half, features), BF),
-            pltpu.VMEM((2, rows, features), BF),
+            pltpu.VMEM((2, 1, rows, features), BF),
             pltpu.VMEM((2, line + 1, half, features), BF),
             pltpu.VMEM((2, rows, features), BF),
             pltpu.VMEM((4, wide, tokens), BF),
@@ -1156,8 +1176,8 @@
             dma((2, chips)),
             dma((2, line)),
             dma((2, line)),
-            dma((2,)),
-            dma((2,)),
+            dma((2, 1)),
+            dma((2, 1)),
             dma((2, line)),
             dma((2, line + 1)),
             dma((2,)),
@@ -1233,7 +1253,7 @@
     count, weight_rows, packed = d_att.shape
     rows, features = tokens.shape
     width, hidden = packed // 4, d_up.shape[2]
-    owners = max(128 // width, count * 16 // rows)
+    owners = max(128 // width, count // 2)
     steps = count // owners
     by_rows = pl.BlockSpec((rows // steps, features), lambda at: (at, 0))
     line = pl.BlockSpec((1, features), lambda at: (0, 0))
@@ -1308,18 +1328,14 @@
     bias_att = jnp.concatenate([bias_att, jnp.zeros((width,), F32)])[None]
     bias_up = lax.dynamic_slice_in_dim(fc1_bias, mine * hidden, hidden, 0)[None]
     if devices == columns and columns % 8 == 0 and width == HEAD and lax.axis_size("tp") == 2:
-        halves = block_order.shape[0]
-        counted = jnp.arange(halves, dtype=jnp.int32)
-        inverse = jnp.sum(
-            jnp.where(block_order[None, :] == counted[:, None], counted[None, :], 0), axis=1
-        )
-        angles = tables(jnp.arange(devices * tokens.shape[0], dtype=jnp.int32), ROT)
-        angles = jnp.concatenate(angles, axis=1)
+        freqs = 10000.0 ** (-np.arange(0, ROT, 2, dtype=np.float32) / ROT)
+        angles = np.arange(devices * tokens.shape[0], dtype=np.float32)[:, None] * freqs[None, :]
+        angles = jnp.asarray(np.concatenate([np.cos(angles), np.sin(angles)], axis=1), F32)
         (
             x_all, g_all, w_att, w_up, w_down, normed, qkvs, lse, attended_t, attended, activated,
-            upward, grad_att,
+            upward, grad_att, inverse,
         ) = collect(
-            block_order, inverse, tokens, cotangent, qkv_weight, out_weight, fc1_weight, fc2_weight,
+            block_order, tokens, cotangent, qkv_weight, out_weight, fc1_weight, fc2_weight,
             ln_gain[None], ln_bias[None], bias_att, bias_up, angles,
         )
         parts = spread(

time: 309 us -> 275 us (0.89)
  Pallas kernels: 303 us -> 270 us
    pallas_call x1, Pallas kernels: 163 us -> 140 us  [spread(): pl.pallas_call(functools.partial(spread_kernel, line), out_shape=[own, ow...]
    pallas_call x1, Pallas kernels: 130 us -> 124 us  [collect(): pl.pallas_call(functools.partial(collect_kernel, line), out_shape=[shape(...]
    pallas_call x1, Pallas kernels: 9.39 us -> 5.92 us  [finish(): pl.pallas_call(finish_kernel, grid=(steps,), out_shape=[shape(tokens.shap...]
where the time goes in v2:
time: 275 us; the launch traced here: 273 us
  Pallas kernels  270 us (98%)
    pallas_call x1, Pallas kernels, spread(): pl.pallas_call(functools.partial(spread_kernel, line), out_shape=[own, ow...  140 us
    pallas_call x1, Pallas kernels, collect(): pl.pallas_call(functools.partial(collect_kernel, line), out_shape=[shape(...  124 us
    pallas_call x1, Pallas kernels, finish(): pl.pallas_call(finish_kernel, grid=(steps,), out_shape=[shape(tokens.shap...  5.92 us

profile of v2, /device:TPU:0, one launch (start us, length us, event | category | flops | bytes accessed | tf_op | source)
XLA Modules:
  0.0 273.3 jit_solution(4699507581925416397)
XLA Ops:
  0.6 0.0 copy-start
  0.7 1.3 dynamic_slice.7
  2.0 0.0 copy-done
  2.0 0.1 constant_dynamic-slice_fusion
  2.1 0.1 reshape.25
  2.2 0.6 concatenate.3
  2.7 124.2 %shard_map.212 = (bf16[2048,2048]{1,0:T(8,128)(2,1)}, bf16[2048,2048]{1,0:T(8,128)(2,1)}, bf16[2048,256]{1,0:T(8,128)(2,1)}, bf16[2048,256]{1,0:T(8,128)(2,1)}, ...) custom-call(s32[32]{0:T(128)} %order_ref.3, ...), custom_call_target="tpu_custom_call" | custom-call | tf_op jit(solution)/shard_map/pallas_call | solution.py:548
  127.0 140.3 %shard_map.213 = (bf16[128,2048]{1,0:T(8,128)(2,1)}, bf16[128,2048]{1,0:T(8,128)(2,1)}, bf16[16,128,256]{2,1,0:T(8,128)(2,1)}, bf16[16,128,256]{2,1,0:T(8,128)(2...) custom-call(s32[32]{0:T(128)} %order_ref.3, ...), custom_call_target="tpu_custom_call" | custom-call | tf_op jit(solution)/shard_map/pallas_call | solution.py:1129
  267.2 5.9 %shard_map.214 = (f32[128,2048]{1,0:T(8,128)}, f32[128,2048]{1,0:T(8,128)}, f32[3,128,1024]{2,1,0:T(8,128)}, f32[128,1024]{1,0:T(8,128)}, f32[128,4096]{1,0:T(8,...) custom-call(bf16[128,2048]{1,0:T(8,128)(2,1)} %tok_ref.3, ...), custom_call_target="tpu_custom_call" | custom-call | tf_op jit(solution)/shard_map/pallas_call | solution.py:1273
Async XLA Ops:
  0.6 1.4 copy-start

commit v3 on v2

--- a/solution.py
+++ b/solution.py
@@ -157,8 +157,8 @@
 def flipped(value, mask, bits):
     result = 0
     for bit in range(bits):
-        part = (value // 2**bit) % 2
-        result = result + 2**bit * (1 - part if mask >> bit & 1 else part)
+        one, other = (value // 2**bit) % 2, (mask // 2**bit) % 2
+        result = result + 2**bit * (one + other - 2 * one * other)
     return result
 
 
@@ -167,10 +167,21 @@
         self.place, self.chunk, self.received = place, chunk, received
         self.send, self.receive, self.own = send, receive, own
         self.count = 4 * place.line
-        bits = self.count.bit_length() - 1
-        self.partners = [
-            (mask, flipped(place.me, mask, bits)) for mask in range(self.count - 1, 0, -1)
-        ]
+        self.bits = self.count.bit_length() - 1
+        self.partners = [self.partner(mask) for mask in range(self.count - 1, 0, -1)]
+
+    def partner(self, mask):
+        return mask, flipped(self.place.me, mask, self.bits)
+
+    def chip(self, turn):
+        return flipped(self.place.me // 2, self.count // 2 - 1 - turn, self.bits - 1)
+
+    def start_chip(self, pieces, turn):
+        mask = self.count - 2 - 2 * turn
+        for n in pieces:
+            self.copy(self.partner(mask + 1), n, False).start()
+            pl.when(mask > 0)(lambda n=n: self.copy(self.partner(mask), n, False).start())
+            pl.when(mask == 0)(lambda n=n: self.kept(n).start())
 
     def copy(self, partner, n, came):
         mask, to = partner
@@ -393,6 +404,13 @@
     quarter = tokens // inverse_ref.shape[0]
     quarters = block // quarter
 
+    shared = batt_ref[:, at_rows(place.me // 2 * 2 * width, 2 * width)]
+    shared = jnp.where(c == 0, shared[:, :width], shared[:, width:])
+    bias_att = jnp.concatenate(
+        [shared[kind : kind + 1] for kind in range(3)] + [jnp.zeros((1, width), F32)], axis=1
+    )
+    bias_up = bup_ref[:, at_rows(place.me * hidden, hidden)]
+
     def project(at, carry):
         here = at_rows(at * block, block)
 
@@ -404,7 +422,7 @@
             part = pl.ds(start, piece)
             unit = (load(start) - mean) * inv_std
             normed_s[here, part] = (unit * gain_ref[:, part] + shift_ref[:, part]).astype(BF)
-        mixed = mm(normed_s[here, :], watt_s[...]) + batt_ref[...]
+        mixed = mm(normed_s[here, :], watt_s[...]) + bias_att
         mixed_s[pl.ds(at * quarters, quarters)] = mixed.reshape(quarters, quarter, 4 * width)
         return carry
 
@@ -503,7 +521,7 @@
 
     def feed(at, carry):
         here = at_rows(at * block, block)
-        upward = mm(normed_s[here, :], wup_s[...]) + bup_ref[...]
+        upward = mm(normed_s[here, :], wup_s[...]) + bias_up
         upward_ref[here, :] = upward
         act_ref[here, :] = (0.5 * upward * (1.0 + gelu_parts(upward))).astype(BF)
         return carry
@@ -602,10 +620,10 @@
 
 
 def spread_kernel(
-    line, order_ref, inverse_ref, att_ref, act_ref, watt_ref, wdown_ref, lse_ref, angle_ref,
-    upward_in, gatt_in, qkvs_in, attt_in, wup_in, normed_ref, g_ref, x_ref,
+    line, order_ref, inverse_ref, att_ref, act_ref, lse_ref, angle_ref,
+    watt_in, wdown_in, upward_in, gatt_in, qkvs_in, attt_in, wup_in, normed_ref, g_ref, x_ref,
     sum_ref, gsum_ref, ratt_ref, rup_ref, rdown_ref, rbias_ref, norms_ref, total_ref,
-    upward_ref, gatt_ref, qkvs_ref, attt_ref, wup_ref,
+    weights_s, upward_ref, gatt_ref, qkvs_ref, attt_ref,
     fresh, own, from_core, from_other, from_across, from_beyond, from_line, done, turned_s, dsend, cols,
     buf, gain_s, shift_s, nsend, nfrom, nline, bias_s, gmix_s, gup_s, kt_s, dkv_s, gm_s,
     in_sem, cols_sem, buf_sem, csend, creceive, credit, ysend, yreceive, xsend, xreceive, bsend,
@@ -627,12 +645,18 @@
     ring = from_core.shape[0]
     shortcuts = tuple(range(line - from_beyond.shape[1], line))
     place.greet()
+    wide, hidden = watt_in.shape[1], wup_in.shape[1]
     late = [
         pltpu.make_async_copy(source, target, in_sem.at[n])
         for n, (source, target) in enumerate(
             (
-                (upward_in, upward_ref), (gatt_in, gatt_ref), (qkvs_in, qkvs_ref), (attt_in, attt_ref),
-                (wup_in, wup_ref),
+                (wdown_in, weights_s.at[:, pl.ds(0, hidden)]),
+                (watt_in, weights_s.at[:, pl.ds(hidden, wide)]),
+                (upward_in, upward_ref),
+                (gatt_in, gatt_ref),
+                (qkvs_in, qkvs_ref),
+                (attt_in, attt_ref),
+                (wup_in, weights_s.at[:, pl.ds(hidden + wide, hidden)]),
             )
         )
     ]
@@ -703,8 +727,10 @@
 
     def columns_of(n, source):
         return Stream(
-            lambda chip, slot: pltpu.make_async_copy(
-                source.at[:, at_rows(chip * pair, pair)], cols.at[n, slot], cols_sem.at[n, slot]
+            lambda at, slot: pltpu.make_async_copy(
+                source.at[:, at_rows(weights.chip(at) * pair, pair)],
+                cols.at[n, slot],
+                cols_sem.at[n, slot],
             ),
             cols.shape[1],
             chips,
@@ -729,9 +755,9 @@
         _, chip = order(turn)
         here = at_rows(chip * block, block)
         fresh_at = lax.rem(turn, 2)
-        left = ((att_ref, act_ref), (gmix_s, gup_s))[t]
-        right = ((watt_ref, wdown_ref), (watt_ref, wup_ref))[t]
-        first, second = left[0][here, :], left[1][here, :]
+        left = ((act_ref, att_ref), (gmix_s, gup_s))[t]
+        left = jnp.concatenate([left[0][here, :], left[1][here, :]], axis=1)
+        right = pl.ds((0, hidden)[t], hidden + wide)
         if t == 1:
             slot = x_rows.step(turn)
 
@@ -741,7 +767,7 @@
             mean, inv_std = row_stats(load, block, features, piece)
         for start in range(0, features, piece):
             part = pl.ds(start, piece)
-            value = mm(first, right[0][part, :], NT) + mm(second, right[1][part, :], NT)
+            value = mm(left, weights_s[part, right], NT)
             fresh[fresh_at, :, part] = value.astype(BF)
             if t == 1:
                 unit = (load(start) - mean) * inv_std
@@ -848,15 +874,9 @@
             lreceive.at[other if came else a], (place.index(other, b, c), y),
         )
 
+    for operand in late[:2]:
+        operand.wait()
     product(0, 0)
-
-    def first_sum(turn, carry):
-        product(0, turn)
-        stage_core(0, turn - 1)
-        return carry
-
-    lax.fori_loop(1, chips, first_sum, 0)
-    stage_core(0, chips - 1)
 
     def turn_over(pieces):
         def one(at, carry):
@@ -870,20 +890,26 @@
     turn_over(((2, att_ref), (3, act_ref)))
     ones = jnp.ones((8, tokens), BF)
 
-    def gradients_down(chip, carry):
-        slot = g_columns.step(chip)
-        here = at_rows(chip * pair, pair)
+    def gradients_down(turn):
+        slot = g_columns.step(turn)
+        here = at_rows(weights.chip(turn) * pair, pair)
         by_grad = cols[1, slot]
         dsend[2, here, :] = mm(turned_s[3], by_grad).T.astype(BF)
         dsend[0, here, :] = mm(turned_s[2], by_grad).T.astype(BF)
         total_ref[:, here] = mm(ones, by_grad)
-        return carry
-
-    lax.fori_loop(0, chips, gradients_down, 0)
-    weights.keep((2,))
-    weights.start((2,))
-
-    late[0].wait()
+        weights.start_chip((2,), turn)
+
+    def first_sum(turn, carry):
+        product(0, turn)
+        stage_core(0, turn - 1)
+        gradients_down(turn - 1)
+        return carry
+
+    lax.fori_loop(1, chips, first_sum, 0)
+    stage_core(0, chips - 1)
+    gradients_down(chips - 1)
+
+    late[2].wait()
 
     def feed_back(at, carry):
         slot = g_rows.step(at)
@@ -893,7 +919,7 @@
         slope = 0.5 * (1.0 + tanh) + 0.5 * upward * (1.0 - tanh * tanh) * (
             math.sqrt(2.0 / math.pi) * (1.0 + 3 * 0.044715 * upward * upward)
         )
-        gup_s[here, :] = (mm(buf[slot], wdown_ref[...]) * slope).astype(BF)
+        gup_s[here, :] = (mm(buf[slot], weights_s[:, pl.ds(0, hidden)]) * slope).astype(BF)
         return carry
 
     lax.fori_loop(0, blocks, feed_back, 0)
@@ -902,22 +928,22 @@
 
     turn_over(((1, gup_s),))
 
-    def gradients_up(chip, carry):
-        slot = normed_columns.step(chip)
-        dsend[1, at_rows(chip * pair, pair), :] = mm(turned_s[1], cols[0, slot]).T.astype(BF)
+    def gradients_up(turn, carry):
+        slot = normed_columns.step(turn)
+        here = at_rows(weights.chip(turn) * pair, pair)
+        dsend[1, here, :] = mm(turned_s[1], cols[0, slot]).T.astype(BF)
+        weights.start_chip((1,), turn)
         return carry
 
     lax.fori_loop(0, chips, gradients_up, 0)
-    weights.keep((1,))
-    weights.start((1,))
     stage_other(0, 1)
     normed_columns.prime()
-    for operand in late[1:]:
+    for operand in late[3:]:
         operand.wait()
 
     quarter = tokens // inverse_ref.shape[0]
     quarters = block // quarter
-    wide = 2 * block
+    span = 2 * block
     scale = 1.0 / math.sqrt(HEAD)
 
     def prepare(at, carry):
@@ -930,50 +956,52 @@
     lax.fori_loop(0, blocks, prepare, 0)
 
     def backward(at, carry):
-        here = at_rows(at * block, block)
+        here = at_rows(at * span, span)
         query = qkvs_ref[here, :][:, :HEAD]
         grad = jnp.concatenate(
-            [gatt_ref[inverse_ref[at * quarters + n]] for n in range(quarters)], axis=0
-        )
-        left = lax.broadcasted_iota(jnp.int32, (block, 2 * HEAD), 1) < HEAD
+            [gatt_ref[inverse_ref[at * 2 * quarters + n]] for n in range(2 * quarters)], axis=0
+        )
+        left = lax.broadcasted_iota(jnp.int32, (span, 2 * HEAD), 1) < HEAD
         grad_wide = grad[:, 2 * HEAD :].astype(F32)
         grad_right = jnp.where(left, 0.0, grad_wide).astype(BF)
         query_left = jnp.concatenate([query, jnp.zeros_like(query)], axis=1)
+        beside_each = jnp.concatenate([query_left, grad_right], axis=0)
         grad = grad[:, 3 * HEAD :]
         delta = jnp.sum(grad_wide.T[HEAD:] * attt_ref[:, here], axis=0, keepdims=True)
         lse = lse_ref[0:1, here]
 
         def back(place_at, query_grad, masked):
-            there = at_rows(place_at * wide, wide)
+            there = at_rows(place_at * span, span)
             keyvalue = qkvs_ref[there, :]
             scores = mm(keyvalue[:, HEAD : 2 * HEAD], query, NT)
             if masked:
-                scores = jnp.where(seen(place_at * wide, at * block, wide, block), scores, NEG)
+                scores = jnp.where(seen(0, 0, span, span), scores, NEG)
             prob = jnp.exp(scores - lse)
             dprob = mm(keyvalue[:, 2 * HEAD : 3 * HEAD], grad, NT)
             dscore = (prob * (dprob - delta)).astype(BF)
-            dkv_s[there, :] += mm(dscore, query_left) + mm(prob.astype(BF), grad_right)
+            dkv_s[there, :] += mm(
+                jnp.concatenate([dscore, prob.astype(BF)], axis=1), beside_each
+            )
             return query_grad + mm(kt_s[:, there], dscore)
 
-        last = at // 2
         query_grad = lax.fori_loop(
-            0, last, lambda n, total: back(n, total, False), jnp.zeros((HEAD, block), F32)
-        )
-        query_grad = back(last, query_grad, True)
+            0, at, lambda n, total: back(n, total, False), jnp.zeros((HEAD, span), F32)
+        )
+        query_grad = back(at, query_grad, True)
         query_grad = jnp.concatenate([query_grad, query_grad], axis=0).T[:, :HEAD]
         query_grad = turned(
             query_grad * scale, angle_ref[here, : ROT // 2], -angle_ref[here, ROT // 2 :]
         ).astype(BF)
-        gm_s[pl.ds(at * quarters, quarters), :, pl.ds(0, HEAD)] = query_grad.reshape(
-            quarters, quarter, HEAD
-        )
-        return carry
-
-    lax.fori_loop(0, blocks // 2, backward, 0)
+        gm_s[pl.ds(at * 2 * quarters, 2 * quarters), :, pl.ds(0, HEAD)] = query_grad.reshape(
+            2 * quarters, quarter, HEAD
+        )
+        return carry
+
+    lax.fori_loop(0, blocks // 4, backward, 0)
     stage_beyond(0)
     for nth in range(2, line - 1):
         stage_other(0, nth)
-    lax.fori_loop(blocks // 2, blocks, backward, 0)
+    lax.fori_loop(blocks // 4, blocks // 2, backward, 0)
     if line > 2:
         stage_other(0, line - 1)
 
@@ -1020,12 +1048,15 @@
     gain_s[...] = jnp.zeros_like(gain_s)
     shift_s[...] = jnp.zeros_like(shift_s)
 
-    def gradients_att(chip):
-        slot = normed_columns.step(chip)
-        here = at_rows(chip * pair, pair)
+    def gradients_att(turn, carry):
+        slot = normed_columns.step(turn)
+        here = at_rows(weights.chip(turn) * pair, pair)
         more = mm(turned_s[0], cols[0, slot]).T
         dsend[0, here, :] = (dsend[0, here, :].astype(F32) + more).astype(BF)
-
+        weights.start_chip((0, 3), turn)
+        return carry
+
+    lax.fori_loop(0, chips, gradients_att, 0)
     product(1, 0)
 
     def second_sum(turn, carry):
@@ -1033,44 +1064,37 @@
         stage_core(1, turn - 1)
         return carry
 
-    def second_sum_too(turn, carry):
-        second_sum(turn, carry)
-        gradients_att(2 * turn - 2)
-        gradients_att(2 * turn - 1)
-        return carry
-
-    lax.fori_loop(1, chips // 2 + 1, second_sum_too, 0)
-    weights.keep((0, 3))
-    weights.start((0, 3))
-    lax.fori_loop(chips // 2 + 1, chips, second_sum, 0)
+    lax.fori_loop(1, chips, second_sum, 0)
     stage_core(1, chips - 1)
     for n, source in enumerate((gain_s, shift_s)):
         total = jnp.sum(source[...], axis=0, keepdims=True)
-        span = features // 4
+        quarter_of = features // 4
         for at in range(4):
-            nsend[0, pl.ds(n * 4 + at, 1), :] = total[:, at * span : (at + 1) * span]
+            nsend[0, pl.ds(n * 4 + at, 1), :] = total[:, at * quarter_of : (at + 1) * quarter_of]
     norm_copy(0).start()
-    stage_beyond(1)
-    for nth in range(line):
-        if nth < line - 1:
-            stage_other(1, nth)
-        stage_line(0, nth)
+    stage_other(1, 0)
+    stage_line(0, 0)
+    stage_line(0, 1)
+    stage_other(1, 1)
+    stage_line(0, 2)
+    stage_line(1, 0)
     norm_copy(0).wait_recv()
     nsend[1] = nsend[0] + nfrom[0]
     norm_copy(1).start()
-    stage_line(1, 0)
+    stage_beyond(1)
+    stage_other(1, 2)
     norm_copy(1).wait_recv()
     nsend[2] = nsend[1] + nfrom[1]
     norm_copy(2).start()
     stage_line(1, 1)
+    stage_line(0, 3)
     norm_copy(2).wait_recv()
     nsend[3] = nsend[2] + nfrom[2]
     nline[a] = nsend[3]
     for other in range(line):
         pl.when(a != other)(lambda other=other: norm_line(other, False).start())
-    stage_other(1, line - 1)
-    for nth in range(2, line):
-        stage_line(1, nth)
+    stage_line(1, 2)
+    stage_line(1, 3)
     for other in range(line):
         pl.when(a != other)(lambda other=other: norm_line(other, True).wait_recv())
     total = nline[0]
@@ -1135,14 +1159,14 @@
             jax.ShapeDtypeStruct((8, features // 4), F32),
             jax.ShapeDtypeStruct((8, features), F32),
         ],
-        in_specs=[smem, smem] + [vmem] * 6 + [hbm] * 8,
+        in_specs=[smem, smem] + [vmem] * 4 + [hbm] * 10,
         out_specs=[vmem, vmem, hbm, hbm, hbm, hbm, vmem, vmem],
         scratch_shapes=[
+            pltpu.VMEM((count * weight_rows, wide + 2 * hidden), BF),
             pltpu.VMEM(upward.shape, F32),
             pltpu.VMEM(grad_att.shape, BF),
             pltpu.VMEM(qkvs.shape, BF),
             pltpu.VMEM(attended_t.shape, F32),
-            pltpu.VMEM(w_up.shape, BF),
             pltpu.VMEM((2, 2 * rows, features), BF),
             pltpu.VMEM((2, chips, rows, features), BF),
             pltpu.VMEM((4, rows, features), BF),
@@ -1166,7 +1190,7 @@
             pltpu.VMEM((HEAD, tokens), BF),
             pltpu.VMEM((tokens, 2 * HEAD), F32),
             pltpu.VMEM((order.shape[0], tokens // order.shape[0], 3 * HEAD), BF),
-            dma((5,)),
+            dma((7,)),
             dma((2, 3)),
             dma((3,)),
             dma((2, chips)),
@@ -1194,7 +1218,7 @@
             collective_id=2, has_side_effects=True, vmem_limit_bytes=63 * 1024 * 1024
         ),
     )(
-        order, inverse, attended, activated, w_att, w_down, lse, angles, upward, grad_att, qkvs,
+        order, inverse, attended, activated, lse, angles, w_att, w_down, upward, grad_att, qkvs,
         attended_t, w_up, normed, g_all, x_all,
     )
 
@@ -1324,9 +1348,6 @@
     mine = myself % columns
     width = qkv_weight.shape[2] // columns
     hidden = fc1_weight.shape[1] // columns
-    bias_att = lax.dynamic_slice_in_dim(qkv_bias, mine * width, width, 1).reshape(-1)
-    bias_att = jnp.concatenate([bias_att, jnp.zeros((width,), F32)])[None]
-    bias_up = lax.dynamic_slice_in_dim(fc1_bias, mine * hidden, hidden, 0)[None]
     if devices == columns and columns % 8 == 0 and width == HEAD and lax.axis_size("tp") == 2:
         freqs = 10000.0 ** (-np.arange(0, ROT, 2, dtype=np.float32) / ROT)
         angles = np.arange(devices * tokens.shape[0], dtype=np.float32)[:, None] * freqs[None, :]
@@ -1336,13 +1357,16 @@
             upward, grad_att, inverse,
         ) = collect(
             block_order, tokens, cotangent, qkv_weight, out_weight, fc1_weight, fc2_weight,
-            ln_gain[None], ln_bias[None], bias_att, bias_up, angles,
+            ln_gain[None], ln_bias[None], qkv_bias, fc1_bias[None], angles,
         )
         parts = spread(
             block_order, inverse, attended, activated, upward, grad_att, qkvs, lse, attended_t, w_att,
             w_up, w_down, angles, normed, g_all, x_all,
         )
     else:
+        bias_att = lax.dynamic_slice_in_dim(qkv_bias, mine * width, width, 1).reshape(-1)
+        bias_att = jnp.concatenate([bias_att, jnp.zeros((width,), F32)])[None]
+        bias_up = lax.dynamic_slice_in_dim(fc1_bias, mine * hidden, hidden, 0)[None]
         parts = by_groups(
             tokens, block_order, ln_gain, ln_bias, qkv_weight, out_weight, fc1_weight, fc2_weight,
             cotangent, bias_att, bias_up,

time: 275 us -> 259 us (0.942)
  Pallas kernels: 270 us -> 258 us
    pallas_call x1, Pallas kernels: 140 us -> 128 us  [spread(): pl.pallas_call(functools.partial(spread_kernel, line), out_shape=[own, ow...]
where the time goes in v3:
time: 259 us
  Pallas kernels  258 us (100%)
    pallas_call x1, Pallas kernels, spread(): pl.pallas_call(functools.partial(spread_kernel, line), out_shape=[own, ow...  128 us
    pallas_call x1, Pallas kernels, collect(): pl.pallas_call(functools.partial(collect_kernel, line), out_shape=[shape(...  124 us
    pallas_call x1, Pallas kernels, finish(): pl.pallas_call(finish_kernel, grid=(steps,), out_shape=[shape(tokens.shap...  5.92 us

profile of v3, /device:TPU:0, one launch (start us, length us, event | category | flops | bytes accessed | tf_op | source)
XLA Modules:
  0.0 258.6 jit_solution(17875139079548033035)
XLA Ops:
  0.6 124.2 %shard_map.212 = (bf16[2048,2048]{1,0:T(8,128)(2,1)}, bf16[2048,2048]{1,0:T(8,128)(2,1)}, bf16[2048,256]{1,0:T(8,128)(2,1)}, bf16[2048,256]{1,0:T(8,128)(2,1)}, ...) custom-call(s32[32]{0:T(128)} %order_ref.3, ...), custom_call_target="tpu_custom_call" | custom-call | tf_op jit(solution)/shard_map/pallas_call | solution.py:566
  124.9 127.6 %shard_map.213 = (bf16[128,2048]{1,0:T(8,128)(2,1)}, bf16[128,2048]{1,0:T(8,128)(2,1)}, bf16[16,128,256]{2,1,0:T(8,128)(2,1)}, bf16[16,128,256]{2,1,0:T(8,128)(2...) custom-call(s32[32]{0:T(128)} %order_ref.3, ...), custom_call_target="tpu_custom_call" | custom-call | tf_op jit(solution)/shard_map/pallas_call | solution.py:1153
  252.5 5.9 %shard_map.214 = (f32[128,2048]{1,0:T(8,128)}, f32[128,2048]{1,0:T(8,128)}, f32[3,128,1024]{2,1,0:T(8,128)}, f32[128,1024]{1,0:T(8,128)}, f32[128,4096]{1,0:T(8,...) custom-call(bf16[128,2048]{1,0:T(8,128)(2,1)} %tok_ref.3, ...), custom_call_target="tpu_custom_call" | custom-call | tf_op jit(solution)/shard_map/pallas_call | solution.py:1297

commit v4 on v3

--- a/solution.py
+++ b/solution.py
@@ -387,13 +387,15 @@
 
     for distance in range(1, line):
         along(0, distance)
+        if distance == line - 1:
+            along(1, 0)
         beside(0, distance - 1)
     beside(0, line - 1)
-    along(1, 0)
-    weights.start((0,))
     lax.fori_loop(0, len(ordered), invert, 0)
     for distance in range(1, line - 1):
         along(1, distance)
+        if distance == 1:
+            weights.start((0,))
         beside(1, distance - 1)
     from_other(0)
     complete(0)

time: 259 us -> 254 us (0.981)
  Pallas kernels: 258 us -> 253 us
    pallas_call x1, Pallas kernels: 124 us -> 119 us  [collect(): pl.pallas_call(functools.partial(collect_kernel, line), out_shape=[shape(...]
where the time goes in v4:
time: 254 us
  Pallas kernels  253 us (100%)
    pallas_call x1, Pallas kernels, spread(): pl.pallas_call(functools.partial(spread_kernel, line), out_shape=[own, ow...  128 us
    pallas_call x1, Pallas kernels, collect(): pl.pallas_call(functools.partial(collect_kernel, line), out_shape=[shape(...  119 us
    pallas_call x1, Pallas kernels, finish(): pl.pallas_call(finish_kernel, grid=(steps,), out_shape=[shape(tokens.shap...  5.92 us

profile of v4, /device:TPU:0, one launch (start us, length us, event | category | flops | bytes accessed | tf_op | source)
XLA Modules:
  0.0 253.6 jit_solution(5071861476566726156)
XLA Ops:
  0.6 118.8 %shard_map.212 = (bf16[2048,2048]{1,0:T(8,128)(2,1)}, bf16[2048,2048]{1,0:T(8,128)(2,1)}, bf16[2048,256]{1,0:T(8,128)(2,1)}, bf16[2048,256]{1,0:T(8,128)(2,1)}, ...) custom-call(s32[32]{0:T(128)} %order_ref.3, ...), custom_call_target="tpu_custom_call" | custom-call | tf_op jit(solution)/shard_map/pallas_call | solution.py:568
  119.5 128.1 %shard_map.213 = (bf16[128,2048]{1,0:T(8,128)(2,1)}, bf16[128,2048]{1,0:T(8,128)(2,1)}, bf16[16,128,256]{2,1,0:T(8,128)(2,1)}, bf16[16,128,256]{2,1,0:T(8,128)(2...) custom-call(s32[32]{0:T(128)} %order_ref.3, ...), custom_call_target="tpu_custom_call" | custom-call | tf_op jit(solution)/shard_map/pallas_call | solution.py:1155
  247.5 5.9 %shard_map.214 = (f32[128,2048]{1,0:T(8,128)}, f32[128,2048]{1,0:T(8,128)}, f32[3,128,1024]{2,1,0:T(8,128)}, f32[128,1024]{1,0:T(8,128)}, f32[128,4096]{1,0:T(8,...) custom-call(bf16[128,2048]{1,0:T(8,128)(2,1)} %tok_ref.3, ...), custom_call_target="tpu_custom_call" | custom-call | tf_op jit(solution)/shard_map/pallas_call | solution.py:1299

commit v5 on v4

--- a/solution.py
+++ b/solution.py
@@ -387,16 +387,16 @@
 
     for distance in range(1, line):
         along(0, distance)
-        if distance == line - 1:
+        if distance == line - 2:
             along(1, 0)
         beside(0, distance - 1)
     beside(0, line - 1)
     lax.fori_loop(0, len(ordered), invert, 0)
     for distance in range(1, line - 1):
         along(1, distance)
+        beside(1, distance - 1)
         if distance == 1:
             weights.start((0,))
-        beside(1, distance - 1)
     from_other(0)
     complete(0)
     weights.wait((0,))
@@ -1089,13 +1089,13 @@
     nsend[2] = nsend[1] + nfrom[1]
     norm_copy(2).start()
     stage_line(1, 1)
-    stage_line(0, 3)
+    stage_line(1, 2)
     norm_copy(2).wait_recv()
     nsend[3] = nsend[2] + nfrom[2]
     nline[a] = nsend[3]
     for other in range(line):
         pl.when(a != other)(lambda other=other: norm_line(other, False).start())
-    stage_line(1, 2)
+    stage_line(0, 3)
     stage_line(1, 3)
     for other in range(line):
         pl.when(a != other)(lambda other=other: norm_line(other, True).wait_recv())

time: 254 us -> 253 us (level)
  no operation moved by 1% of the time
where the time goes in v5:
time: 253 us; the launch traced here: 252 us
  Pallas kernels  251 us (99%)
    pallas_call x1, Pallas kernels, spread(): pl.pallas_call(functools.partial(spread_kernel, line), out_shape=[own, ow...  126 us
    pallas_call x1, Pallas kernels, collect(): pl.pallas_call(functools.partial(collect_kernel, line), out_shape=[shape(...  119 us
    pallas_call x1, Pallas kernels, finish(): pl.pallas_call(finish_kernel, grid=(steps,), out_shape=[shape(tokens.shap...  5.92 us

profile of v5, /device:TPU:0, one launch (start us, length us, event | category | flops | bytes accessed | tf_op | source)
XLA Modules:
  0.0 252.2 jit_solution(15955726546582116584)
XLA Ops:
  0.6 119.1 %shard_map.212 = (bf16[2048,2048]{1,0:T(8,128)(2,1)}, bf16[2048,2048]{1,0:T(8,128)(2,1)}, bf16[2048,256]{1,0:T(8,128)(2,1)}, bf16[2048,256]{1,0:T(8,128)(2,1)}, ...) custom-call(s32[32]{0:T(128)} %order_ref.3, ...), custom_call_target="tpu_custom_call" | custom-call | tf_op jit(solution)/shard_map/pallas_call | solution.py:568
  119.7 126.4 %shard_map.213 = (bf16[128,2048]{1,0:T(8,128)(2,1)}, bf16[128,2048]{1,0:T(8,128)(2,1)}, bf16[16,128,256]{2,1,0:T(8,128)(2,1)}, bf16[16,128,256]{2,1,0:T(8,128)(2...) custom-call(s32[32]{0:T(128)} %order_ref.3, ...), custom_call_target="tpu_custom_call" | custom-call | tf_op jit(solution)/shard_map/pallas_call | solution.py:1155
  246.2 5.9 %shard_map.214 = (f32[128,2048]{1,0:T(8,128)}, f32[128,2048]{1,0:T(8,128)}, f32[3,128,1024]{2,1,0:T(8,128)}, f32[128,1024]{1,0:T(8,128)}, f32[128,4096]{1,0:T(8,...) custom-call(bf16[128,2048]{1,0:T(8,128)(2,1)} %tok_ref.3, ...), custom_call_target="tpu_custom_call" | custom-call | tf_op jit(solution)/shard_map/pallas_call | solution.py:1299
